TPU v7x, 128 devices: a whole 4x4x4 slice. The times are simulated.
128 devices in a mesh: pb: 8 (over x, z_lo), ka: 8 (over y, core), ha: 2 (over z_hi).
Axes of the slice: x: 4, y: 4, z: 4 (z_hi: 2, z_lo: 2; z = z_hi * 2 + z_lo), core: 2. Of those that a mesh axis runs over, the one named last changes fastest.
Arguments:
- query_states: bfloat16 [8192, 4096], P(('pb', 'ka'), 'ha'), parts along dimension 1, may hold values from -6 to 6
- key_states: bfloat16 [8192, 2048], P(('ka', 'pb'), 'ha'), parts along dimension 1, may hold values from -6 to 6
- value_states: bfloat16 [8192, 2048], P(('ka', 'pb'), 'ha'), parts along dimension 1, may hold values from -6 to 6
- attn_output: bfloat16 [8192, 4096], P(('pb', 'ka'), 'ha'), parts along dimension 1, may hold values from -6 to 6
- output_grad: bfloat16 [8192, 4096], P(('pb', 'ka'), 'ha'), parts along dimension 1, may hold values from -48 to 48
- logsumexp: float32 [32, 8192], P('ha', ('pb', 'ka')), parts along dimension 0, as said below
- block_order: int32 [32], P('ha'), parts along dimension 0, may hold values from 0 to 15, as said below
- doc_lengths: int32 [8], P('ha'), parts along dimension 0, may hold values from 512 to 4096, as said below
Outputs:
- query_grad: bfloat16 [8192, 4096], P(('pb', 'ka'), 'ha'), parts along dimension 1
- key_grad: bfloat16 [8192, 2048], P(('ka', 'pb'), 'ha'), parts along dimension 1
- value_grad: bfloat16 [8192, 2048], P(('ka', 'pb'), 'ha'), parts along dimension 1
There are 2 independent parts, one for each index of `ha`. A program takes and returns all parts, laid end to end along the dimension named above; each array names one. Nothing has to cross between parts.
Inputs may be any that keep to these rules, and one draw needn't show every extreme that they name: `block_order`: slots 2i and 2i + 1 hold blocks b and 15 - b for some b; every block stands in one slot. `doc_lengths`: the lengths sum to 8192. logsumexp[h, r] minus the log of the number of positions of its document up to and including row r's position lies between -0.5 and 1.5.
All inputs are finite; a program needn't handle non-finite values.
Results may differ from a plain program's by a relative error of at most 0.0051.
Values may be sent and summed in bfloat16 or wider, within the bound.
A program may use at most 128 MiB of HBM per device.

v0:
```python
from functools import partial

import jax
import jax.numpy as jnp
from jax import lax
from jax.sharding import PartitionSpec as P

QH = 2


softcap = 50.0
score_scale = 144.0 ** (-0.5)


def row_sums(grads, saved, heads):
    count = grads.shape[0]
    return jnp.sum(
        grads.reshape(count, heads, -1).astype(jnp.float32)
        * saved.reshape(count, heads, -1).astype(jnp.float32),
        axis=2,
    ).T


def segment_of(positions, ends):
    return jnp.sum((positions[:, None] >= ends[None, :]).astype(jnp.int32), axis=1)


def tile_update(
    state,
    query_rows,
    grad_rows,
    lse_rows,
    delta_rows,
    key_rows,
    value_rows,
    allowed,
    query_half,
    key_half,
):
    span = query_rows.shape[0]
    heads = lse_rows.shape[0]
    width = query_rows.shape[1] // heads

    def per_head(head_index, carry):
        acc_query, acc_key, acc_value = carry
        column = head_index * width
        kv_column = head_index // QH * width
        query_head = lax.dynamic_slice_in_dim(query_rows, column, width, 1)
        grad_head = lax.dynamic_slice_in_dim(grad_rows, column, width, 1)
        key_head = lax.dynamic_slice_in_dim(key_rows, kv_column, width, 1)
        value_head = lax.dynamic_slice_in_dim(value_rows, kv_column, width, 1)
        lse_head = lax.dynamic_index_in_dim(lse_rows, head_index, 0, keepdims=False)
        delta_head = lax.dynamic_index_in_dim(delta_rows, head_index, 0, keepdims=False)
        raw = jnp.dot(query_head, key_head.T, preferred_element_type=jnp.float32) * score_scale
        capped = softcap * jnp.tanh(raw / softcap)
        prob = jnp.where(allowed, jnp.exp(capped - lse_head[:, None]), jnp.float32(0.0))
        prob_low = prob.astype(jnp.bfloat16)
        dprob = jnp.dot(grad_head, value_head.T, preferred_element_type=jnp.float32)
        ratio = capped / softcap
        dscore = (
            prob * (dprob - delta_head[:, None]) * (1.0 - ratio * ratio) * score_scale
        ).astype(jnp.bfloat16)
        corner = (query_half * span, column)
        previous = lax.dynamic_slice(acc_query, corner, (span, width))
        fresh = jnp.dot(dscore, key_head, preferred_element_type=jnp.float32)
        acc_query = lax.dynamic_update_slice(acc_query, previous + fresh, corner)
        kv_corner = (key_half * span, kv_column)
        old_key = lax.dynamic_slice(acc_key, kv_corner, (span, width))
        old_value = lax.dynamic_slice(acc_value, kv_corner, (span, width))
        acc_key = lax.dynamic_update_slice(
            acc_key,
            old_key + jnp.dot(dscore.T, query_head, preferred_element_type=jnp.float32),
            kv_corner,
        )
        acc_value = lax.dynamic_update_slice(
            acc_value,
            old_value + jnp.dot(prob_low.T, grad_head, preferred_element_type=jnp.float32),
            kv_corner,
        )
        return (acc_query, acc_key, acc_value)

    return lax.fori_loop(0, heads, per_head, state)


def body(
    query_states,
    key_states,
    value_states,
    attn_output,
    output_grad,
    logsumexp,
    block_order,
    doc_lengths,
):
    heads = logsumexp.shape[0]
    query_all, grad_all, saved_all = (
        lax.all_gather(query_states, "ka", axis=0, tiled=True),
        lax.all_gather(output_grad, "ka", axis=0, tiled=True),
        lax.all_gather(attn_output, "ka", axis=0, tiled=True),
    )
    lse_all = lax.all_gather(logsumexp, "ka", axis=1, tiled=True)
    delta_all = row_sums(grad_all, saved_all, heads)
    keys_all, values_all = (
        lax.all_gather(key_states, "pb", axis=0, tiled=True),
        lax.all_gather(value_states, "pb", axis=0, tiled=True),
    )
    span = query_all.shape[0] // 2
    kv_width = keys_all.shape[1]
    row_slot = lax.axis_index("pb")
    col_slot = lax.axis_index("ka")
    ends = jnp.cumsum(doc_lengths)
    offsets = jnp.arange(span, dtype=jnp.int32)
    query_pos = [block_order[2 * row_slot + half_index] * span + offsets for half_index in (0, 1)]
    key_pos = [block_order[2 * col_slot + half_index] * span + offsets for half_index in (0, 1)]
    query_seg = [segment_of(positions, ends) for positions in query_pos]
    key_seg = [segment_of(positions, ends) for positions in key_pos]
    state = (
        jnp.zeros((2 * span, query_all.shape[1]), jnp.float32),
        jnp.zeros((2 * span, kv_width), jnp.float32),
        jnp.zeros((2 * span, kv_width), jnp.float32),
    )
    for query_half in (0, 1):
        for key_half in (0, 1):
            allowed = (key_pos[key_half][None, :] <= query_pos[query_half][:, None]) & (
                key_seg[key_half][None, :] == query_seg[query_half][:, None]
            )
            needed = jnp.logical_and(
                block_order[2 * col_slot + key_half] <= block_order[2 * row_slot + query_half],
                key_seg[key_half][span - 1] >= query_seg[query_half][0],
            )
            update = partial(
                tile_update,
                query_rows=query_all[query_half * span : (query_half + 1) * span],
                grad_rows=grad_all[query_half * span : (query_half + 1) * span],
                lse_rows=lse_all[:, query_half * span : (query_half + 1) * span],
                delta_rows=delta_all[:, query_half * span : (query_half + 1) * span],
                key_rows=keys_all[key_half * span : (key_half + 1) * span],
                value_rows=values_all[key_half * span : (key_half + 1) * span],
                allowed=allowed,
                query_half=query_half,
                key_half=key_half,
            )
            state = lax.cond(needed, update, lambda carry: carry, state)
    grad_query, grad_key, grad_value = state
    query_grad = lax.psum_scatter(grad_query, "ka", scatter_dimension=0, tiled=True).astype(
        jnp.bfloat16
    )
    key_sum, value_sum = (
        lax.psum_scatter(grad_key, "pb", scatter_dimension=0, tiled=True),
        lax.psum_scatter(grad_value, "pb", scatter_dimension=0, tiled=True),
    )
    return (query_grad, key_sum.astype(jnp.bfloat16), value_sum.astype(jnp.bfloat16))


def solution(mesh):
    placed = (
        P(("pb", "ka"), "ha"),
        P(("ka", "pb"), "ha"),
        P(("ka", "pb"), "ha"),
        P(("pb", "ka"), "ha"),
        P(("pb", "ka"), "ha"),
        P("ha", ("pb", "ka")),
        P("ha"),
        P("ha"),
    )
    return jax.shard_map(
        body,
        mesh=mesh,
        in_specs=placed,
        out_specs=(P(("pb", "ka"), "ha"), P(("ka", "pb"), "ha"), P(("ka", "pb"), "ha")),
        check_vma=False,
    )
```

profile of v0, /device:TPU:1, one launch (start us, length us, event | category | flops | bytes accessed | tf_op | source)
XLA Modules:
  0.0 926.8 jit_solution(832823506213420846)
XLA Ops:
  28.3 14.8 %all_gather.20 = f32[16,1024]{1,0:T(8,128)S(1)} all-gather(f32[16,128]{1,0:T(8,128)} %param.29), channel_id=1, replica_groups=mesh['pb'=8,'ka'=8,'ha'=2] {'ka'}, dimensions={1}, use_global_device_ids=true | all-gather | bytes 73728 | tf_op jit(solution)/shard_map/all_gather | solution.py:101
  44.0 18.6 %all-gather.8.cloned.1.call-done = bf16[1024,1024]{1,0:T(8,128)(2,1)} async-done(((bf16[128,1024]{1,0:T(8,128)(2,1)}), bf16[1024,1024]{1,0:T(8,128)(2,1)}) %all-gather.8.cloned.1.call-update) | async-done | bytes 2097168 | tf_op jit(solution)/shard_map/all_gather | solution.py:104
  64.3 50.9 %all-gather.12.cloned.1.call-done = bf16[1024,1024]{1,0:T(8,128)(2,1)} async-done(((bf16[128,1024]{1,0:T(8,128)(2,1)}), bf16[1024,1024]{1,0:T(8,128)(2,1)}) %all-gather.12.cloned.1.call-update) | async-done | bytes 2097168 | tf_op jit(solution)/shard_map/all_gather | solution.py:105
  115.2 3.1 fusion.110
  118.3 33.4 %all-gather.10.cloned.1.call-done = bf16[1024,2048]{1,0:T(8,128)(2,1)} async-done(((bf16[128,2048]{1,0:T(8,128)(2,1)}), bf16[1024,2048]{1,0:T(8,128)(2,1)}) %all-gather.10.cloned.1.call-update) | async-done | bytes 4194320 | tf_op jit(solution)/shard_map/all_gather | solution.py:98
  151.7 33.7 %all-gather.14.cloned.1.call-done = bf16[1024,2048]{1,0:T(8,128)(2,1)} async-done(((bf16[128,2048]{1,0:T(8,128)(2,1)}), bf16[1024,2048]{1,0:T(8,128)(2,1)}) %all-gather.14.cloned.1.call-update) | async-done | bytes 4194320 | tf_op jit(solution)/shard_map/all_gather | solution.py:99
  185.4 5.4 multiply_bitcast_fusion
  190.8 5.3 copy.19
  196.0 6.8 reduce_sum.49
  203.9 5.0 fusion.108
  209.0 10.1 %all-gather.6.cloned.1.call-done = bf16[1024,2048]{1,0:T(8,128)(2,1)} async-done(((bf16[128,2048]{1,0:T(8,128)(2,1)}), bf16[1024,2048]{1,0:T(8,128)(2,1)}) %all-gather.6.cloned.1.call-update) | async-done | bytes 4194320 | tf_op jit(solution)/shard_map/all_gather | solution.py:97
  219.0 4.8 fusion.109
  223.9 9.3 %conditional.4 = (f32[1024,2048]{1,0:T(8,128)}, f32[1024,1024]{1,0:T(8,128)}, f32[1024,1024]{1,0:T(8,128)}) conditional(s32[]{:T(128)} %bitcast.17, () %tuple.122, (bf16[512,2048]{1,0:T(8,128)(2,1)}, bf16[512,1024]{1,0:T(8,128)(2,1)S(1)}, f32[16,512]{1,0:T(8,128)S(1)}, pred[512,512]{1,0:T(32,128)(4,1)S(1)}, bf16[512,2048]{1,0:T(8,128)(2,1)}, ...), branch_computations={%region_6.7_spmd, %region_7.10_spmd} | conditional | flops 339673088 | bytes 24590896 | solution.py:143
  223.9 4.3 broadcast_in_dim.89
  228.2 2.5 broadcast.200
  230.7 2.5 broadcast.200.clone
  233.2 147.0 %conditional.5 = ((f32[1024,2048]{1,0:T(8,128)}, f32[1024,1024]{1,0:T(8,128)}, f32[1024,1024]{1,0:T(8,128)})) conditional(s32[]{:T(128)} %bitcast.16, (f32[1024,2048]{1,0:T(8,128)}, f32[1024,1024]{1,0:T(8,128)}, f32[1024,1024]{1,0:T(8,128)}) %conditional.4, (bf16[512,2048]{1,0:T(8,128)(2,1)}, bf16[512,1024]{1,0:T(8,128)(2,1)S(1)}, ...), branch_computations={%region_10.11_spmd, %region_11.14_spmd} | conditional | flops 339673088 | bytes 7813675 | solution.py:143
  233.3 146.9 %while.73 = (s32[]{:T(128)}, f32[1024,2048]{1,0:T(8,128)}, f32[1024,1024]{1,0:T(8,128)}, f32[1024,1024]{1,0:T(8,128)}, bf16[512,2048]{1,0:T(8,128)(2,1)}, /*inde...) while((s32[]{:T(128)}, f32[1024,2048]{1,0:T(8,128)}, ...), condition=%wide.region_13.13_spmd, body=%wide.region_12.12_spmd.sunk | while | flops 339673088 | bytes 7747963 | solution.py:82
  240.2 2.3 fusion.227
  249.3 2.3 fusion.227
  276.8 2.3 fusion.227
  286.0 2.3 fusion.227
  295.1 2.3 fusion.227
  304.4 2.3 fusion.227
  313.6 2.3 fusion.227
  331.9 2.3 fusion.227
  341.1 2.3 fusion.227
  368.6 2.3 fusion.227
  377.8 2.3 fusion.227
  383.1 385.9 %reduce-scatter.6.cloned.1.call-done = f32[128,1024]{1,0:T(8,128)} async-done(((f32[1024,1024]{1,0:T(8,128)}), f32[128,1024]{1,0:T(8,128)}) %reduce-scatter.6.cloned.1.call-update) | async-done | bytes 524304 | tf_op jit(solution)/shard_map/reduce_scatter | solution.py:149
  770.8 91.9 %reduce-scatter.8.cloned.1.call-done = f32[128,1024]{1,0:T(8,128)} async-done(((f32[1024,1024]{1,0:T(8,128)}), f32[128,1024]{1,0:T(8,128)}) %reduce-scatter.8.cloned.1.call-update) | async-done | bytes 524304 | tf_op jit(solution)/shard_map/reduce_scatter | solution.py:150
  864.4 53.4 %reduce-scatter.4.cloned.1.call-done = f32[128,2048]{1,0:T(8,128)} async-done(((f32[1024,2048]{1,0:T(8,128)}), f32[128,2048]{1,0:T(8,128)}) %reduce-scatter.4.cloned.1.call-update) | async-done | bytes 1048592 | tf_op jit(solution)/shard_map/reduce_scatter | solution.py:145
  (125 shorter events, 141.5 us)
Async XLA Ops:
  7.2 55.5 %all-gather.8.cloned.1.call-start = ((), (), s32[]{:S(2)}) async-start(), calls=%async_computation.4 | async-start | bytes 2359296 | tf_op jit(solution)/shard_map/all_gather | solution.py:104
  7.9 107.3 %all-gather.12.cloned.1.call-start = ((), (), s32[]{:S(2)}) async-start(), calls=%async_computation.6 | async-start | bytes 2359296 | tf_op jit(solution)/shard_map/all_gather | solution.py:105
  8.6 143.1 %all-gather.10.cloned.1.call-start = ((), (), s32[]{:S(2)}) async-start(), calls=%async_computation.5 | async-start | bytes 4718592 | tf_op jit(solution)/shard_map/all_gather | solution.py:98
  9.4 176.0 %all-gather.14.cloned.1.call-start = ((), (), s32[]{:S(2)}) async-start(), calls=%async_computation.7 | async-start | bytes 4718592 | tf_op jit(solution)/shard_map/all_gather | solution.py:99
  10.0 209.1 %all-gather.6.cloned.1.call-start = ((), (), s32[]{:S(2)}) async-start(), calls=%async_computation.3 | async-start | bytes 4718592 | tf_op jit(solution)/shard_map/all_gather | solution.py:97
  10.5 758.4 %reduce-scatter.6.cloned.1.call-start = ((), (), s32[]{:S(2)}) async-start(), calls=%async_computation.9 | async-start | bytes 4718592 | tf_op jit(solution)/shard_map/reduce_scatter | solution.py:149
  203.9 176.2 %copy-start = (f32[16,512]{0,1:T(8,128)}, f32[16,512]{0,1:T(8,128)S(1)}, u32[]{:S(2)}) copy-start(f32[16,512]{0,1:T(8,128)S(1)} %get-tuple-element.1433) | copy-start | bytes 98308
  381.6 481.1 %reduce-scatter.8.cloned.1.call-start = ((), (), s32[]{:S(2)}) async-start(), calls=%async_computation.10 | async-start | bytes 4718592 | tf_op jit(solution)/shard_map/reduce_scatter | solution.py:150
  382.3 535.6 %reduce-scatter.4.cloned.1.call-start = ((), (), s32[]{:S(2)}) async-start(), calls=%async_computation.8 | async-start | bytes 9437184 | tf_op jit(solution)/shard_map/reduce_scatter | solution.py:145
Sparse Core Ops, SparseCore 0:
  9.6 52.9 all-gather.7
  64.3 50.9 all-gather.11
  116.9 34.7 all-gather.9
  153.3 32.0 all-gather.13
  186.9 32.0 all-gather.5
  381.7 387.2 reduce-scatter.5
  771.4 91.2 reduce-scatter.7
  865.1 52.7 reduce-scatter.3
where the time goes:
time: 933 us; the launch traced here: 927 us
  waiting for transfers between devices  682 us (73%)
  matrix products  146 us (16%)
  local copies, waits for them, and re-layouts  35.7 us (4%)
  between operations  27.3 us (3%)
  other arithmetic  19.6 us (2%)
  blocking collectives  14.8 us (2%)
    reduce_scatter x1, waiting for transfers between devices, body(): lax.psum_scatter(grad_key, 'pb', scatter_dimension=0, tiled=True)  386 us
    reduce_scatter x1, waiting for transfers between devices, body(): lax.psum_scatter(grad_value, 'pb', scatter_dimension=0, tiled=True)  91.9 us
    reduce_scatter x1, waiting for transfers between devices, body(): lax.psum_scatter(grad_query, 'ka', scatter_dimension=0, tiled=True)  53.4 us
    all_gather x1, waiting for transfers between devices, body(): lax.all_gather(value_states, 'pb', axis=0, tiled=True)  50.9 us
    dot_general x16, matrix products, per_head(): jnp.dot(prob_low.T, grad_head, preferred_element_type=jnp.float32)  36.5 us
    all_gather x1, waiting for transfers between devices, body(): lax.all_gather(attn_output, 'ka', axis=0, tiled=True)  33.7 us
    all_gather x1, waiting for transfers between devices, body(): lax.all_gather(output_grad, 'ka', axis=0, tiled=True)  33.4 us
    dot_general x16, matrix products, per_head(): jnp.dot(dscore.T, query_head, preferred_element_type=jnp.float32)  33.4 us
  transfers between devices with their start and end apart: 8, of which 8 were waited for; matrix products, arithmetic and copies ran while one was open for 4% of the time, Pallas kernels for 0%

commit v1 on v0

v1 whole, which is shorter than its diff:
```python
from functools import partial
import math

import jax
import jax.numpy as jnp
from jax import lax
from jax.experimental import pallas as pl
from jax.experimental.pallas import tpu as pltpu
from jax.sharding import PartitionSpec as P

HD = 128
BLK = 512
ROWS = 128
NX, NY = 4, 4
BF16 = jnp.bfloat16
F32 = jnp.float32

softcap = 50.0
score_scale = 144.0 ** (-0.5)
log2e = math.log2(math.e)

Y_ORDER = (0, 1, 3, 2)


def place():
    pb, ka = lax.axis_index("pb"), lax.axis_index("ka")
    return pb // 2, pb % 2, ka // 2, ka % 2


def device(x, z, y, c):
    return {"pb": 2 * x + z, "ka": 2 * y + c}


def remote(src, dst, send, recv, to):
    return pltpu.make_async_remote_copy(
        src_ref=src,
        dst_ref=dst,
        send_sem=send,
        recv_sem=recv,
        device_id=to,
        device_id_type=pl.DeviceIdType.MESH,
    )


def enter(x, z, y, c):
    barrier = pltpu.get_barrier_semaphore()
    for dy in range(NY):
        for dz in range(2):
            for dc in range(2):
                if (dy, dz, dc) != (0, 0, 0):
                    to = device(x, (z + dz) % 2, (y + dy) % NY, (c + dc) % 2)
                    pl.semaphore_signal(barrier, inc=1, device_id=to, device_id_type=pl.DeviceIdType.MESH)
    for dx in (1, 3):
        to = device((x + dx) % NX, z, y, c)
        pl.semaphore_signal(barrier, inc=1, device_id=to, device_id_type=pl.DeviceIdType.MESH)
    pl.semaphore_wait(barrier, 17)


def columns(head):
    return pl.ds(pl.multiple_of(head * HD, HD), HD)


def rows_at(start, count):
    return pl.ds(pl.multiple_of(start, ROWS), count)


def gather_kernel(
    q_ref, k_ref, v_ref, o_ref, g_ref, lse_ref,
    qh_ref, gh_ref, kv_ref, aux_ref,
    o_v, g_v, aux_v,
    load_sem, kv_send, kv_recv, x_send, x_recv, x2_send, x2_recv, sib_send, sib_recv, q_send, q_recv,
):
    x, z, y, c = place()
    loads = [
        pltpu.make_async_copy(o_ref, o_v, load_sem.at[0]),
        pltpu.make_async_copy(g_ref, g_v, load_sem.at[1]),
    ]
    for load in loads:
        load.start()
    enter(x, z, y, c)

    sibling = device(x, z, y, 1 - c)
    right, left = device((x + 1) % NX, z, y, c), device((x + 3) % NX, z, y, c)
    own_rows = rows_at((2 * y + c) * 1024 + (2 * x + z) * ROWS, ROWS)
    sends = []

    kv_copies = {}
    for dy in Y_ORDER:
        for dz in range(2):
            ty, tz = (y + dy) % NY, (z + dz) % 2
            for part, ref in enumerate((k_ref, v_ref)):
                src = ref.at[:, columns(2 * ty + tz)]
                dst = kv_ref.at[own_rows, pl.ds(part * HD, HD)]
                at = (dy * 2 + dz) * 2 + part
                if dy == 0 and dz == 0:
                    copy = pltpu.make_async_copy(src, dst, kv_recv.at[at])
                else:
                    copy = remote(src, dst, kv_send.at[at], kv_recv.at[at], device(x, tz, ty, c))
                    sends.append(copy)
                copy.start()
                kv_copies[dy, dz, part] = copy

    def kv_block(plane, dy):
        return rows_at((2 * ((y + NY - dy) % NY) + c) * 1024 + 2 * plane * ROWS, 2 * ROWS)

    def to_sibling(step, dy, rows):
        at = step * NY + dy
        copy = remote(kv_ref.at[rows, :], kv_ref.at[rows, :], sib_send.at[at], sib_recv.at[at], sibling)
        copy.start()
        sends.append(copy)
        return copy

    first, sib, q_copies = {}, [], []
    for dy in Y_ORDER:
        for dz in range(2):
            for part in range(2):
                copy = kv_copies[dy, dz, part]
                if dy == 0 and dz == 0:
                    copy.wait()
                else:
                    copy.wait_recv()
        rows = kv_block(x, dy)
        for way, to in ((0, right), (1, left)):
            at = way * NY + dy
            copy = remote(kv_ref.at[rows, :], kv_ref.at[rows, :], x_send.at[at], x_recv.at[at], to)
            copy.start()
            sends.append(copy)
            first[way, dy] = copy
        sib.append(to_sibling(0, dy, rows))
        for dz in range(2):
            for dc in range(2):
                ty, tz, tc = (y + dy) % NY, (z + dz) % 2, (c + dc) % 2
                head = 2 * (2 * ty + tz) + tc
                for part, (ref, out) in enumerate(((q_ref, qh_ref), (g_ref, gh_ref))):
                    src = ref.at[:, columns(head)]
                    dst = out.at[rows_at(z * 1024 + (2 * y + c) * ROWS, ROWS), :]
                    at = ((dy * 2 + dz) * 2 + dc) * 3 + part
                    if (dy, dz, dc) == (0, 0, 0):
                        copy = pltpu.make_async_copy(src, dst, q_recv.at[at])
                    else:
                        copy = remote(src, dst, q_send.at[at], q_recv.at[at], device(x, tz, ty, tc))
                        sends.append(copy)
                    copy.start()
                    q_copies.append(copy)

    for load in loads:
        load.wait()
    for h in range(16):
        cols = pl.ds(h * HD, HD)
        prod = g_v[:, cols].astype(F32) * o_v[:, cols].astype(F32)
        delta = jnp.sum(prod.T, axis=0, keepdims=True)
        lse = lse_ref[h : h + 1, :] * log2e
        aux_v[h] = jnp.concatenate([lse, delta, jnp.zeros((6, ROWS), F32)], axis=0)
    for dy in Y_ORDER:
        for dz in range(2):
            for dc in range(2):
                ty, tz, tc = (y + dy) % NY, (z + dz) % 2, (c + dc) % 2
                head = 2 * (2 * ty + tz) + tc
                src = aux_v.at[head]
                dst = aux_ref.at[z * 8 + 2 * y + c]
                at = ((dy * 2 + dz) * 2 + dc) * 3 + 2
                if (dy, dz, dc) == (0, 0, 0):
                    copy = pltpu.make_async_copy(src, dst, q_recv.at[at])
                else:
                    copy = remote(src, dst, q_send.at[at], q_recv.at[at], device(x, tz, ty, tc))
                    sends.append(copy)
                copy.start()
                q_copies.append(copy)

    second = {}
    for dy in Y_ORDER:
        for way, (plane, to) in enumerate((((x + 3) % NX, right), ((x + 1) % NX, left))):
            first[way, dy].wait_recv()
            rows = kv_block(plane, dy)
            at = way * NY + dy
            part = kv_ref.at[rows, pl.ds(way * HD, HD)]
            copy = remote(part, part, x2_send.at[at], x2_recv.at[at], to)
            copy.start()
            sends.append(copy)
            second[way, dy] = copy
            sib.append(to_sibling(1 + way, dy, rows))
    for dy in Y_ORDER:
        second[0, dy].wait_recv()
        second[1, dy].wait_recv()
        sib.append(to_sibling(3, dy, kv_block((x + 2) % NX, dy)))
    for index, copy in enumerate(q_copies):
        if index < 2 or index == 32:
            copy.wait()
        else:
            copy.wait_recv()
    for copy in sib:
        copy.wait_recv()
    for copy in sends:
        copy.wait_send()


def gather(q, k, v, o, g, lse):
    hbm = pl.BlockSpec(memory_space=pl.ANY)
    dma = pltpu.SemaphoreType.DMA
    return pl.pallas_call(
        gather_kernel,
        out_shape=(
            jax.ShapeDtypeStruct((2048, HD), BF16),
            jax.ShapeDtypeStruct((2048, HD), BF16),
            jax.ShapeDtypeStruct((8192, 2 * HD), BF16),
            jax.ShapeDtypeStruct((16, 8, ROWS), F32),
        ),
        in_specs=[hbm] * 5 + [pl.BlockSpec(memory_space=pltpu.VMEM)],
        out_specs=(hbm,) * 4,
        scratch_shapes=[
            pltpu.VMEM((ROWS, 2048), BF16),
            pltpu.VMEM((ROWS, 2048), BF16),
            pltpu.VMEM((16, 8, ROWS), F32),
            dma((2,)),
            dma((16,)), dma((16,)),
            dma((8,)), dma((8,)),
            dma((8,)), dma((8,)),
            dma((16,)), dma((16,)),
            dma((48,)), dma((48,)),
        ],
        compiler_params=pltpu.CompilerParams(collective_id=0, has_side_effects=True, vmem_limit_bytes=32 << 20),
        name="gather_heads",
    )(q, k, v, o, g, lse)


def nt(a, b):
    return lax.dot_general(a, b, (((1,), (1,)), ((), ())), preferred_element_type=F32)


def tn(a, b):
    return lax.dot_general(a, b, (((0,), (0,)), ((), ())), preferred_element_type=F32)


def tile_kernel(
    order_ref, lens_ref, q_ref, g_ref, kv_ref, aux_ref,
    dq_ref, dkv_ref,
    acc_q, acc_kv, rows_f, rows_i,
):
    x = lax.axis_index("pb") // 2
    starts = [lens_ref[0], lens_ref[0] + lens_ref[1], lens_ref[0] + lens_ref[1] + lens_ref[2]]

    def low_of(p):
        low = jnp.zeros_like(p)
        for start in starts:
            low = jnp.where(p >= start, start, low)
        return low

    acc_q[...] = jnp.zeros_like(acc_q)
    query_block = [order_ref[4 * x + i] for i in range(4)]
    query_low = [low_of(query_block[i] * BLK) for i in range(4)]
    for i in range(4):
        for part in range(2):
            rows_f[i, part : part + 1, :] = jnp.concatenate(
                [aux_ref[4 * i + j, part : part + 1, :] for j in range(4)], axis=1
            )
        pos = query_block[i] * BLK + lax.broadcasted_iota(jnp.int32, (1, BLK), 1)
        rows_i[i, 0:1, :] = pos
        rows_i[i, 1:2, :] = low_of(pos)

    def key_step(slot, _):
        key_block = order_ref[slot]
        key_row = pl.multiple_of(slot * BLK, BLK)
        acc_kv[...] = jnp.zeros_like(acc_kv)
        for i in range(4):
            needed = jnp.logical_and(key_block <= query_block[i], key_block * BLK + (BLK - 1) >= query_low[i])

            @pl.when(needed)
            def _():
                q = q_ref[i * BLK : (i + 1) * BLK, :]
                g = g_ref[i * BLK : (i + 1) * BLK, :]
                lse, delta = rows_f[i, 0:1, :], rows_f[i, 1:2, :]
                qpos, qlow = rows_i[i, 0:1, :], rows_i[i, 1:2, :]
                for sub in range(2):
                    size = BLK // 2
                    off = sub * size
                    k = kv_ref[pl.ds(key_row + off, size), 0:HD]
                    v = kv_ref[pl.ds(key_row + off, size), HD : 2 * HD]
                    kpos = key_block * BLK + off + lax.broadcasted_iota(jnp.int32, (size, BLK), 0)
                    allowed = (kpos <= qpos) & (kpos >= qlow)
                    t = jnp.tanh(nt(k, q) * (score_scale / softcap))
                    p = jnp.where(allowed, jnp.exp2(t * (softcap * log2e) - lse), 0.0)
                    ds = p * (nt(v, g) - delta) * ((1.0 - t * t) * score_scale)
                    ds = ds.astype(BF16)
                    acc_kv[off : off + size, 0:HD] += jnp.dot(ds, q, preferred_element_type=F32)
                    acc_kv[off : off + size, HD : 2 * HD] += jnp.dot(
                        p.astype(BF16), g, preferred_element_type=F32
                    )
                    acc_q[i * BLK : (i + 1) * BLK, :] += tn(ds, k)

        dkv_ref[pl.ds(key_row, BLK), :] = acc_kv[...].astype(BF16)
        return 0

    lax.fori_loop(0, 16, key_step, 0)
    dq_ref[...] = acc_q[...].astype(BF16)


def tiles(order, lens, q, g, kv, aux):
    smem = pl.BlockSpec(memory_space=pltpu.SMEM)
    vmem = pl.BlockSpec(memory_space=pltpu.VMEM)
    return pl.pallas_call(
        tile_kernel,
        out_shape=(
            jax.ShapeDtypeStruct((2048, HD), BF16),
            jax.ShapeDtypeStruct((8192, 2 * HD), BF16),
        ),
        in_specs=[smem, smem] + [vmem] * 4,
        out_specs=(vmem, vmem),
        scratch_shapes=[
            pltpu.VMEM((2048, HD), F32),
            pltpu.VMEM((BLK, 2 * HD), F32),
            pltpu.VMEM((4, 8, BLK), F32),
            pltpu.VMEM((4, 8, BLK), jnp.int32),
        ],
        compiler_params=pltpu.CompilerParams(vmem_limit_bytes=48 << 20),
        name="tiles",
    )(order, lens, q, g, kv, aux)


def scatter_kernel(
    dq_ref, dkv_ref,
    dq_out, dk_out, dv_out,
    own, sib, send2, land2, send1, land1, fin,
    own_sem, sib_send, sib_recv, s2_send, s2_recv, s1_send, s1_recv, f_send, f_recv, q_send, q_recv,
):
    x, z, y, c = place()
    head = 2 * y + z
    enter(x, z, y, c)
    sibling = device(x, z, y, 1 - c)
    right, left = device((x + 1) % NX, z, y, c), device((x + 3) % NX, z, y, c)
    planes = [(x + 2) % NX, (x + 1) % NX, (x + 3) % NX, x]
    ys = [(y + dy) % NY for dy in (2, 1, 3, 0)]
    sends = []

    own_copies, sib_copies = {}, {}
    for r, plane in enumerate(planes):
        for n, ty in enumerate(ys):
            at = r * NY + n
            copy = remote(
                dkv_ref.at[ty, 1 - c, plane], sib.at[r, n], sib_send.at[at], sib_recv.at[at], sibling
            )
            copy.start()
            sends.append(copy)
            sib_copies[r, n] = copy
            copy = pltpu.make_async_copy(dkv_ref.at[ty, c, plane], own.at[r, n], own_sem.at[at])
            copy.start()
            own_copies[r, n] = copy

    q_copies = []
    for dy in Y_ORDER:
        for dz in range(2):
            for dc in range(2):
                ty, tz, tc = (y + dy) % NY, (z + dz) % 2, (c + dc) % 2
                src = dq_ref.at[rows_at(tz * 1024 + (2 * ty + tc) * ROWS, ROWS), :]
                dst = dq_out.at[:, columns(2 * head + c)]
                at = (dy * 2 + dz) * 2 + dc
                if at == 0:
                    copy = pltpu.make_async_copy(src, dst, q_recv.at[at])
                else:
                    copy = remote(src, dst, q_send.at[at], q_recv.at[at], device(x, tz, ty, tc))
                    sends.append(copy)
                copy.start()
                q_copies.append(copy)

    def arrived(r, n):
        own_copies[r, n].wait()
        sib_copies[r, n].wait_recv()

    def pair_sum(r, n, part):
        cols = pl.ds(part * HD, HD)
        return own[r, n, :, cols].astype(F32) + sib[r, n, :, cols].astype(F32)

    copies2 = {}
    for n in range(NY):
        arrived(0, n)
        for part, to in enumerate((right, left)):
            send2[part, n] = pair_sum(0, n, part).astype(BF16)
            at = part * NY + n
            copy = remote(send2.at[part, n], land2.at[part, n], s2_send.at[at], s2_recv.at[at], to)
            copy.start()
            sends.append(copy)
            copies2[part, n] = copy

    copies1 = {}

    def send_on(way, n, part, to):
        at = (way * 2 + part) * NY + n
        copy = remote(send1.at[way, part, n], land1.at[way, part, n], s1_send.at[at], s1_recv.at[at], to)
        copy.start()
        sends.append(copy)
        copies1[way, part, n] = copy

    for n in range(NY):
        for way, to in enumerate((right, left)):
            arrived(1 + way, n)
            part = 1 - way
            send1[way, part, n] = pair_sum(1 + way, n, part).astype(BF16)
            send_on(way, n, part, to)
    for n in range(NY):
        for way, to in enumerate((right, left)):
            part = way
            copies2[part, n].wait_recv()
            send1[way, part, n] = (pair_sum(1 + way, n, part) + land2[part, n].astype(F32)).astype(BF16)
            send_on(way, n, part, to)

    f_copies = []
    for n in range(NY):
        arrived(3, n)
        for part, out in ((0, dk_out), (1, dv_out)):
            for way in range(2):
                copies1[way, part, n].wait_recv()
            total = pair_sum(3, n, part) + land1[0, part, n].astype(F32) + land1[1, part, n].astype(F32)
            fin[part, n] = total.astype(BF16)
            for dz in range(2):
                tz = (z + dz) % 2
                src = fin.at[part, n, rows_at(tz * ROWS, ROWS), :]
                dst = out.at[:, columns(head)]
                at = (n * 2 + part) * 2 + dz
                if n == NY - 1 and dz == 0:
                    copy = pltpu.make_async_copy(src, dst, f_recv.at[at])
                    copy.start()
                    f_copies.append((True, copy))
                else:
                    copy = remote(src, dst, f_send.at[at], f_recv.at[at], device(x, tz, ys[n], c))
                    copy.start()
                    sends.append(copy)
                    f_copies.append((False, copy))

    for index, copy in enumerate(q_copies):
        if index == 0:
            copy.wait()
        else:
            copy.wait_recv()
    for local, copy in f_copies:
        if local:
            copy.wait()
        else:
            copy.wait_recv()
    for copy in sends:
        copy.wait_send()


def scatter(dq, dkv):
    hbm = pl.BlockSpec(memory_space=pl.ANY)
    dma = pltpu.SemaphoreType.DMA
    return pl.pallas_call(
        scatter_kernel,
        out_shape=(
            jax.ShapeDtypeStruct((ROWS, 2048), BF16),
            jax.ShapeDtypeStruct((ROWS, 1024), BF16),
            jax.ShapeDtypeStruct((ROWS, 1024), BF16),
        ),
        in_specs=[hbm] * 2,
        out_specs=(hbm,) * 3,
        scratch_shapes=[
            pltpu.VMEM((4, NY, 256, 256), BF16),
            pltpu.VMEM((4, NY, 256, 256), BF16),
            pltpu.VMEM((2, NY, 256, HD), BF16),
            pltpu.VMEM((2, NY, 256, HD), BF16),
            pltpu.VMEM((2, 2, NY, 256, HD), BF16),
            pltpu.VMEM((2, 2, NY, 256, HD), BF16),
            pltpu.VMEM((2, NY, 256, HD), BF16),
            dma((16,)),
            dma((16,)), dma((16,)),
            dma((8,)), dma((8,)),
            dma((16,)), dma((16,)),
            dma((16,)), dma((16,)),
            dma((16,)), dma((16,)),
        ],
        compiler_params=pltpu.CompilerParams(collective_id=1, has_side_effects=True, vmem_limit_bytes=32 << 20),
        name="scatter_grads",
    )(dq, dkv)


def body(
    query_states,
    key_states,
    value_states,
    attn_output,
    output_grad,
    logsumexp,
    block_order,
    doc_lengths,
):
    q, g, kv, aux = gather(query_states, key_states, value_states, attn_output, output_grad, logsumexp)
    dq, dkv = tiles(block_order, doc_lengths, q, g, kv, aux)
    return scatter(dq, dkv.reshape(NY, 2, NX, 256, 2 * HD))


def solution(mesh):
    placed = (
        P(("pb", "ka"), "ha"),
        P(("ka", "pb"), "ha"),
        P(("ka", "pb"), "ha"),
        P(("pb", "ka"), "ha"),
        P(("pb", "ka"), "ha"),
        P("ha", ("pb", "ka")),
        P("ha"),
        P("ha"),
    )
    return jax.shard_map(
        body,
        mesh=mesh,
        in_specs=placed,
        out_specs=(P(("pb", "ka"), "ha"), P(("ka", "pb"), "ha"), P(("ka", "pb"), "ha")),
        check_vma=False,
    )
```

time: 933 us -> 105 us (0.11)
  waiting for transfers between devices: 682 us -> 0 us
  matrix products: 146 us -> 0 us
  Pallas kernels: 0 us -> 93 us
  between operations: 27.3 us -> 0.68 us
  local copies, waits for them, and re-layouts: 35.7 us -> 11.2 us
  other arithmetic: 19.6 us -> 0 us
  blocking collectives: 14.8 us -> 0 us
    reduce_scatter x3 -> x0, waiting for transfers between devices: 531 us -> none  [the longest x1 386 us: body(): lax.psum_scatter(grad_key, 'pb', scatter_dimension=0, tiled=True)]
    all_gather x5 -> x0, waiting for transfers between devices: 147 us -> none  [the longest x1 50.9 us: body(): lax.all_gather(value_states, 'pb', axis=0, tiled=True)]
    dot_general x80 -> x0, matrix products: 146 us -> none  [the longest x16 36.5 us: per_head(): jnp.dot(prob_low.T, grad_head, preferred_element_type=jnp.float32)]
    pallas_call x0 -> x3, Pallas kernels: none -> 93 us  [the longest x1 42.3 us: scatter(): pl.pallas_call(scatter_kernel, out_shape=(jax.ShapeDtypeStruct((ROWS, 204...]
    slice x10 -> x0, local copies, waits for them, and re-layouts: 17.9 us -> none  [the longest x1 5.03 us: body(): grad_all[query_half * span:(query_half + 1) * span]]
    all_gather x1 -> x0, blocking collectives: 14.8 us -> none  [body(): lse_all = lax.all_gather(logsumexp, 'ka', axis=1, tiled=True)]
  transfers between devices with their start and end apart: 8 -> 0, of which waited for: 8 -> 0; matrix products, arithmetic and copies ran while one was open for 4% -> 0% of each run, Pallas kernels for 0% -> 0%
where the time goes in v1:
time: 105 us
  Pallas kernels  93 us (89%)
  local copies, waits for them, and re-layouts  11.2 us (11%)
    pallas_call x1, Pallas kernels, scatter(): pl.pallas_call(scatter_kernel, out_shape=(jax.ShapeDtypeStruct((ROWS, 204...  42.3 us
    pallas_call x1, Pallas kernels, gather(): pl.pallas_call(gather_kernel, out_shape=(jax.ShapeDtypeStruct((2048, HD),...  32.9 us
    pallas_call x1, Pallas kernels, tiles(): pl.pallas_call(tile_kernel, out_shape=(jax.ShapeDtypeStruct((2048, HD), B...  17.8 us
    unnamed x21, local copies, waits for them, and re-layouts  11.2 us

profile of v1, /device:TPU:1, one launch (start us, length us, event | category | flops | bytes accessed | tf_op | source)
XLA Modules:
  0.0 104.8 jit_solution(8438520441333141323)
XLA Ops:
  0.6 0.0 copy-start.1
  0.6 1.0 copy-done.1
  1.7 0.0 copy-start.2
  1.7 1.0 copy-done.2
  2.7 0.0 copy-start.3
  2.7 1.0 copy-done.3
  3.8 0.0 copy-start.4
  3.8 0.9 copy-done.4
  4.7 0.0 copy-start.5
  4.7 0.9 copy-done.5
  5.7 0.0 copy-start.6
  5.7 0.7 copy-done.6
  6.4 32.9 %gather_heads.1 = (bf16[2048,128]{1,0:T(8,128)(2,1)S(1)}, bf16[2048,128]{1,0:T(8,128)(2,1)S(1)}, bf16[8192,256]{1,0:T(8,128)(2,1)S(1)}, f32[16,8,128]{2,1,0:T(8,128)S(1)}) custom-call(bf16[128,2048]{1,0:T(8,128)(2,1)S(1)} %copy-done.1, bf16[128,1024]{1,0:T(8,128)(2,1)S(1)} %copy-done.4, bf16[128,1024]{1,0:T(8,128)(2,1)S(1)} %copy-done.5, ...), custom_call_target="tpu_custom_call" | custom-call | tf_op jit(solution)/shard_map/gather_heads/pallas_call | solution.py:200
  39.3 0.0 copy-start
  39.3 1.9 %copy-done = bf16[8192,256]{1,0:T(8,128)(2,1)} copy-done((bf16[8192,256]{1,0:T(8,128)(2,1)}, bf16[8192,256]{1,0:T(8,128)(2,1)S(1)}, u32[]{:S(2)}) %copy-start) | copy-done | bytes 4194328
  41.2 0.0 copy-start.7
  41.2 0.7 copy-done.7
  41.9 0.0 copy-start.8
  41.9 0.7 copy-done.8
  42.5 17.8 %tiles.1 = (bf16[2048,128]{1,0:T(8,128)(2,1)S(1)}, bf16[8192,256]{1,0:T(8,128)(2,1)S(1)}) custom-call(s32[16]{0:T(128)S(1)} %copy-done.7, s32[4]{0:T(128)S(1)} %copy-done.8, bf16[2048,128]{1,0:T(8,128)(2,1)S(1)} %get-tuple-element.9.q_ref, bf16[2048,128]{1,0:T(8,128)(2,1)S(1)} %get-tuple-element.10.g_ref, bf16[8192,256]{1,0:T(8,128)(2,1)} %copy-done, ...), custom_call_target="tpu_custom_call" | custom-call | tf_op jit(solution)/shard_map/tiles/pallas_call | solution.py:300
  60.3 42.3 %scatter_grads.1 = (bf16[128,2048]{1,0:T(8,128)(2,1)S(1)}, bf16[128,1024]{1,0:T(8,128)(2,1)S(1)}, bf16[128,1024]{1,0:T(8,128)(2,1)S(1)}) custom-call(bf16[2048,128]{1,0:T(8,128)(2,1)S(1)} %get-tuple-element.13.dq_ref, bf16[4,2,4,256,256]{4,3,2,1,0:T(8,128)(2,1)S(1)} %bitcast.1), custom_call_target="tpu_custom_call" | custom-call | tf_op jit(solution)/shard_map/scatter_grads/pallas_call | solution.py:445
  102.6 0.8 copy.14
  103.4 0.7 copy.15
  104.1 0.7 copy.16
Async XLA Ops:
  0.6 1.0 copy-start.1
  1.7 1.0 copy-start.2
  2.7 1.0 copy-start.3
  3.8 0.9 copy-start.4
  4.7 0.9 copy-start.5
  5.7 0.7 copy-start.6
  39.3 2.0 %copy-start = (bf16[8192,256]{1,0:T(8,128)(2,1)}, bf16[8192,256]{1,0:T(8,128)(2,1)S(1)}, u32[]{:S(2)}) copy-start(bf16[8192,256]{1,0:T(8,128)(2,1)S(1)} %get-tuple-element.11.kv_ref) | copy-start | bytes 12582916
  41.2 0.7 copy-start.7
  41.9 0.7 copy-start.8

commit v2 on v1

v2 whole, which is shorter than its diff:
```python
from functools import partial
import math

import jax
import jax.numpy as jnp
from jax import lax
from jax.experimental import pallas as pl
from jax.experimental.pallas import tpu as pltpu
from jax.sharding import PartitionSpec as P

HD = 128
BLK = 512
ROWS = 128
NX, NY = 4, 4
VMEM_LIMIT = 60 << 20
BF16 = jnp.bfloat16
F32 = jnp.float32

softcap = 50.0
score_scale = 144.0 ** (-0.5)
log2e = math.log2(math.e)

ORDER = (0, 1, 3, 2)
QT = 256


def place():
    pb, ka = lax.axis_index("pb"), lax.axis_index("ka")
    return pb // 2, pb % 2, ka // 2, ka % 2


def device(x, z, y, c):
    return {"pb": 2 * x + z, "ka": 2 * y + c}


def remote(src, dst, send, recv, to):
    return pltpu.make_async_remote_copy(
        src_ref=src,
        dst_ref=dst,
        send_sem=send,
        recv_sem=recv,
        device_id=to,
        device_id_type=pl.DeviceIdType.MESH,
    )


def enter(x, z, y, c):
    barrier = pltpu.get_barrier_semaphore()
    for dx in range(NX):
        for dz in range(2):
            for dc in range(2):
                if (dx, dz, dc) != (0, 0, 0):
                    to = device((x + dx) % NX, (z + dz) % 2, y, (c + dc) % 2)
                    pl.semaphore_signal(barrier, inc=1, device_id=to, device_id_type=pl.DeviceIdType.MESH)
    for dy in (1, 3):
        to = device(x, z, (y + dy) % NY, c)
        pl.semaphore_signal(barrier, inc=1, device_id=to, device_id_type=pl.DeviceIdType.MESH)
    pl.semaphore_wait(barrier, 17)


def columns(head):
    return pl.ds(pl.multiple_of(head * HD, HD), HD)


def rows_at(start, count):
    return pl.ds(pl.multiple_of(start, ROWS), count)


def gather_kernel(
    q_ref, k_ref, v_ref, o_ref, g_ref, lse_ref,
    qh_ref, gh_ref, qt_ref, gt_ref, lb_ref, db_ref, kv_ref,
    o_v, g_v, aux_v, qh_v, gh_v, auxh_v, qt_v, gt_v, lb_v, db_v,
    load_sem, kv_send, kv_recv, y_send, y_recv, y2_send, y2_recv, sib_send, sib_recv, q_send, q_recv, out_sem,
):
    x, z, y, c = place()
    loads = [
        pltpu.make_async_copy(o_ref, o_v, load_sem.at[0]),
        pltpu.make_async_copy(g_ref, g_v, load_sem.at[1]),
    ]
    for load in loads:
        load.start()
    enter(x, z, y, c)

    sibling = device(x, z, y, 1 - c)
    up, down = device(x, z, (y + 1) % NY, c), device(x, z, (y + 3) % NY, c)
    own_rows = rows_at((2 * y + c) * 1024 + (2 * x + z) * ROWS, ROWS)
    sends = []

    kv_copies = {}
    for dx in ORDER:
        for dz in range(2):
            tx, tz = (x + dx) % NX, (z + dz) % 2
            for part, ref in enumerate((k_ref, v_ref)):
                src = ref.at[:, columns(2 * tx + tz)]
                dst = kv_ref.at[own_rows, pl.ds(part * HD, HD)]
                at = (dx * 2 + dz) * 2 + part
                if dx == 0 and dz == 0:
                    copy = pltpu.make_async_copy(src, dst, kv_recv.at[at])
                else:
                    copy = remote(src, dst, kv_send.at[at], kv_recv.at[at], device(tx, tz, y, c))
                    sends.append(copy)
                copy.start()
                kv_copies[dx, dz, part] = copy

    def kv_block(plane, dx):
        return rows_at((2 * plane + c) * 1024 + ((x + NX - dx) % NX) * 2 * ROWS, 2 * ROWS)

    def to_sibling(step, dx, rows):
        at = step * NX + dx
        copy = remote(kv_ref.at[rows, :], kv_ref.at[rows, :], sib_send.at[at], sib_recv.at[at], sibling)
        copy.start()
        sends.append(copy)
        return copy

    def each_target(dx):
        for dz in range(2):
            for dc in range(2):
                tx, tz, tc = (x + dx) % NX, (z + dz) % 2, (c + dc) % 2
                yield (dx * 2 + dz) * 2 + dc, 2 * (2 * tx + tz) + tc, device(tx, tz, y, tc)

    first, sib, q_copies, q_local = {}, [], [], []

    def head_copy(src, dst, at, sem, to):
        if at == 0:
            copy = pltpu.make_async_copy(src, dst, q_recv.at[sem])
            q_local.append(copy)
        else:
            copy = remote(src, dst, q_send.at[sem], q_recv.at[sem], to)
            sends.append(copy)
            q_copies.append(copy)
        copy.start()

    for dx in ORDER:
        for dz in range(2):
            for part in range(2):
                copy = kv_copies[dx, dz, part]
                if dx == 0 and dz == 0:
                    copy.wait()
                else:
                    copy.wait_recv()
        rows = kv_block(y, dx)
        for way, to in ((0, up), (1, down)):
            at = way * NX + dx
            copy = remote(kv_ref.at[rows, :], kv_ref.at[rows, :], y_send.at[at], y_recv.at[at], to)
            copy.start()
            sends.append(copy)
            first[way, dx] = copy
        sib.append(to_sibling(0, dx, rows))
        for at, head, to in each_target(dx):
            for part, (ref, out) in enumerate(((q_ref, qh_v), (g_ref, gh_v))):
                src = ref.at[:, columns(head)]
                dst = out.at[2 * x + z, rows_at(c * ROWS, ROWS), :]
                head_copy(src, dst, at, at * 3 + part, to)

    for load in loads:
        load.wait()
    for h in range(16):
        cols = pl.ds(h * HD, HD)
        prod = g_v[:, cols].astype(F32) * o_v[:, cols].astype(F32)
        delta = jnp.sum(prod.T, axis=0, keepdims=True)
        lse = lse_ref[h : h + 1, :] * log2e
        aux_v[h] = jnp.concatenate([lse, delta, jnp.zeros((6, ROWS), F32)], axis=0)
    for dx in ORDER:
        for at, head, to in each_target(dx):
            head_copy(aux_v.at[head], auxh_v.at[2 * (2 * x + z) + c], at, at * 3 + 2, to)

    second = {}
    for dx in ORDER:
        for way, (plane, to) in enumerate((((y + 3) % NY, up), ((y + 1) % NY, down))):
            first[way, dx].wait_recv()
            rows = kv_block(plane, dx)
            at = way * NX + dx
            part = kv_ref.at[rows, pl.ds(way * HD, HD)]
            copy = remote(part, part, y2_send.at[at], y2_recv.at[at], to)
            copy.start()
            sends.append(copy)
            second[way, dx] = copy
            sib.append(to_sibling(1 + way, dx, rows))

    for copy in q_local:
        copy.wait()
    for copy in q_copies:
        copy.wait_recv()
    outs = [
        pltpu.make_async_copy(qh_v, qh_ref, out_sem.at[0]),
        pltpu.make_async_copy(gh_v, gh_ref, out_sem.at[1]),
    ]
    for i in range(8):
        qt_v[i] = qh_v[i].T
        gt_v[i] = gh_v[i].T
    for i in range(16):
        for row, out in ((0, lb_v), (1, db_v)):
            out[i] = jnp.broadcast_to(auxh_v[i, row : row + 1, :], (ROWS, ROWS)).T
    outs += [
        pltpu.make_async_copy(qt_v, qt_ref, out_sem.at[2]),
        pltpu.make_async_copy(gt_v, gt_ref, out_sem.at[3]),
        pltpu.make_async_copy(lb_v, lb_ref, out_sem.at[4]),
        pltpu.make_async_copy(db_v, db_ref, out_sem.at[5]),
    ]
    for copy in outs:
        copy.start()

    for dx in ORDER:
        second[0, dx].wait_recv()
        second[1, dx].wait_recv()
        sib.append(to_sibling(3, dx, kv_block((y + 2) % NY, dx)))
    for copy in sib:
        copy.wait_recv()
    for copy in sends:
        copy.wait_send()
    for copy in outs:
        copy.wait()


def gather(q, k, v, o, g, lse):
    hbm = pl.BlockSpec(memory_space=pl.ANY)
    dma = pltpu.SemaphoreType.DMA
    half = jax.ShapeDtypeStruct((8, QT, HD), BF16)
    turned = jax.ShapeDtypeStruct((8, HD, QT), BF16)
    spread = jax.ShapeDtypeStruct((16, ROWS, ROWS), F32)
    return pl.pallas_call(
        gather_kernel,
        out_shape=(half, half, turned, turned, spread, spread, jax.ShapeDtypeStruct((8192, 2 * HD), BF16)),
        in_specs=[hbm] * 5 + [pl.BlockSpec(memory_space=pltpu.VMEM)],
        out_specs=(hbm,) * 7,
        scratch_shapes=[
            pltpu.VMEM((ROWS, 2048), BF16),
            pltpu.VMEM((ROWS, 2048), BF16),
            pltpu.VMEM((16, 8, ROWS), F32),
            pltpu.VMEM((8, QT, HD), BF16),
            pltpu.VMEM((8, QT, HD), BF16),
            pltpu.VMEM((16, 8, ROWS), F32),
            pltpu.VMEM((8, HD, QT), BF16),
            pltpu.VMEM((8, HD, QT), BF16),
            pltpu.VMEM((16, ROWS, ROWS), F32),
            pltpu.VMEM((16, ROWS, ROWS), F32),
            dma((2,)),
            dma((16,)), dma((16,)),
            dma((8,)), dma((8,)),
            dma((8,)), dma((8,)),
            dma((16,)), dma((16,)),
            dma((48,)), dma((48,)),
            dma((6,)),
        ],
        compiler_params=pltpu.CompilerParams(collective_id=0, has_side_effects=True, vmem_limit_bytes=VMEM_LIMIT),
        name="gather_heads",
    )(q, k, v, o, g, lse)


def nt(a, b):
    return lax.dot_general(a, b, (((1,), (1,)), ((), ())), preferred_element_type=F32)


def nn(a, b):
    return jnp.dot(a, b, preferred_element_type=F32)


def tile_kernel(
    order_ref, lens_ref, qh_ref, gh_ref, qt_ref, gt_ref, lb_ref, db_ref, kv_ref,
    dq_ref, dkv_ref,
    q_v, g_v, qt_v, gt_v, lb_v, db_v, kv_v, acc_q, acc_k, acc_v, dq_v, dkv_v,
    s_a, s_b, dp_a, dp_b, p_a, p_b, ds_a, ds_b, tile_q, tile_k, tile_at, tile_cut, sems,
):
    y = lax.axis_index("ka") // 2
    loads = [
        pltpu.make_async_copy(src, dst, sems.at[n])
        for n, (src, dst) in enumerate(
            ((qh_ref, q_v), (gh_ref, g_v), (kv_ref, kv_v), (lb_ref, lb_v), (db_ref, db_v), (qt_ref, qt_v), (gt_ref, gt_v))
        )
    ]
    for load in loads:
        load.start()
    starts = [lens_ref[0], lens_ref[0] + lens_ref[1], lens_ref[0] + lens_ref[1] + lens_ref[2]]

    def low_of(p):
        low = jnp.zeros_like(p)
        for start in starts:
            low = jnp.where(p >= start, start, low)
        return low

    base = [order_ref[2 * i + y // 2] * BLK + (y % 2) * QT for i in range(8)]
    first_low = [low_of(base[i]) for i in range(8)]
    last_low = [low_of(base[i] + (QT - 1)) for i in range(8)]

    def list_slot(slot, count):
        key = order_ref[slot] * BLK
        for i in range(8):
            needed = jnp.logical_and(key < base[i] + QT, key + BLK > first_low[i])
            whole = jnp.logical_and(key + BLK <= base[i] + 1, key >= last_low[i])
            tile_q[count] = i
            tile_k[count] = slot
            tile_at[count] = key - base[i]
            tile_cut[count] = jnp.where(whole, 0, 1)
            count = count + needed.astype(jnp.int32)
        return count

    count = lax.fori_loop(0, 16, list_slot, 0)
    tile_q[count] = 0
    tile_k[count] = 0
    tile_at[count] = 1 << 20
    tile_cut[count] = 1
    pairs = (count + 1) // 2
    last = 2 * pairs - 1

    acc_q[...] = jnp.zeros_like(acc_q)

    def clear(slot, _):
        acc_k[slot] = jnp.zeros((HD, BLK), F32)
        acc_v[slot] = jnp.zeros((HD, BLK), F32)
        return 0

    lax.fori_loop(0, 16, clear, 0)
    for load in loads:
        load.wait()

    def scores(t, s_ref, dp_ref):
        i, rows = tile_q[t], pl.ds(pl.multiple_of(tile_k[t] * BLK, BLK), BLK)
        s_ref[...] = nt(q_v[i], kv_v[rows, 0:HD])
        dp_ref[...] = nt(g_v[i], kv_v[rows, HD : 2 * HD])

    def weigh(t, s_ref, dp_ref, p_ref, ds_ref, cut):
        i, at = tile_q[t], tile_at[t]
        if cut:
            query_base = order_ref[2 * i + y // 2] * BLK + (y % 2) * QT
        step = 16
        for r in range(0, QT, step):
            j, rr = r // ROWS, r % ROWS
            lse = lb_v[2 * i + j, rr : rr + step, :]
            delta = db_v[2 * i + j, rr : rr + step, :]
            lse = jnp.concatenate([lse] * (BLK // HD), axis=1)
            delta = jnp.concatenate([delta] * (BLK // HD), axis=1)
            th = jnp.tanh(s_ref[r : r + step, :] * (score_scale / softcap))
            p = jnp.exp2(th * (softcap * log2e) - lse)
            if cut:
                row = lax.broadcasted_iota(jnp.int32, (step, HD), 0) + r
                low = low_of(row + query_base) - query_base
                row = jnp.concatenate([row] * (BLK // HD), axis=1)
                low = jnp.concatenate([low] * (BLK // HD), axis=1)
                key = lax.broadcasted_iota(jnp.int32, (step, BLK), 1) + at
                p = jnp.where((key <= row) & (key >= low), p, 0.0)
            ds = p * (dp_ref[r : r + step, :] - delta) * ((1.0 - th * th) * score_scale)
            p_ref[r : r + step, :] = p.astype(BF16)
            ds_ref[r : r + step, :] = ds.astype(BF16)

    def gradients(t, p_ref, ds_ref):
        i, slot = tile_q[t], tile_k[t]
        rows = pl.ds(pl.multiple_of(slot * BLK, BLK), BLK)
        acc_v[slot] += nn(gt_v[i], p_ref[...])
        acc_k[slot] += nn(qt_v[i], ds_ref[...])
        acc_q[i] += nn(ds_ref[...], kv_v[rows, 0:HD])

    buffers = ((s_a, dp_a, p_a, ds_a), (s_b, dp_b, p_b, ds_b))

    def step(t, parity):
        s0, dp0, p0, ds0 = buffers[parity]
        s1, dp1, p1, ds1 = buffers[1 - parity]
        middle = jnp.minimum(t + 1, last)

        def whole_step(cut):
            gradients(t, p0, ds0)
            scores(jnp.minimum(t + 2, last), s0, dp0)
            weigh(middle, s1, dp1, p1, ds1, cut)

        pl.when(tile_cut[middle] == 0)(lambda: whole_step(False))
        pl.when(tile_cut[middle] != 0)(lambda: whole_step(True))

    scores(0, s_a, dp_a)
    scores(1, s_b, dp_b)
    weigh(0, s_a, dp_a, p_a, ds_a, True)

    def pair(n, _):
        step(2 * n, 0)
        step(2 * n + 1, 1)
        return 0

    lax.fori_loop(0, pairs, pair, 0)

    dq_v[...] = acc_q[...].astype(BF16)
    out_q = pltpu.make_async_copy(dq_v, dq_ref, sems.at[0])
    out_q.start()

    def finish(slot, _):
        for half in range(2):
            cols = slice(half * QT, (half + 1) * QT)
            dkv_v[2 * slot + half, 0] = acc_k[slot, :, cols].astype(BF16)
            dkv_v[2 * slot + half, 1] = acc_v[slot, :, cols].astype(BF16)
        return 0

    lax.fori_loop(0, 16, finish, 0)
    out_kv = pltpu.make_async_copy(dkv_v, dkv_ref, sems.at[1])
    out_kv.start()
    out_q.wait()
    out_kv.wait()


def tiles(order, lens, *arrays):
    smem = pl.BlockSpec(memory_space=pltpu.SMEM)
    hbm = pl.BlockSpec(memory_space=pl.ANY)
    wide = pltpu.VMEM((QT, BLK), F32)
    narrow = pltpu.VMEM((QT, BLK), BF16)
    listed = pltpu.SMEM((136,), jnp.int32)
    return pl.pallas_call(
        tile_kernel,
        out_shape=(
            jax.ShapeDtypeStruct((8, QT, HD), BF16),
            jax.ShapeDtypeStruct((32, 2, HD, QT), BF16),
        ),
        in_specs=[smem, smem] + [hbm] * 7,
        out_specs=(hbm, hbm),
        scratch_shapes=[
            pltpu.VMEM((8, QT, HD), BF16),
            pltpu.VMEM((8, QT, HD), BF16),
            pltpu.VMEM((8, HD, QT), BF16),
            pltpu.VMEM((8, HD, QT), BF16),
            pltpu.VMEM((16, ROWS, ROWS), F32),
            pltpu.VMEM((16, ROWS, ROWS), F32),
            pltpu.VMEM((8192, 2 * HD), BF16),
            pltpu.VMEM((8, QT, HD), F32),
            pltpu.VMEM((16, HD, BLK), F32),
            pltpu.VMEM((16, HD, BLK), F32),
            pltpu.VMEM((8, QT, HD), BF16),
            pltpu.VMEM((32, 2, HD, QT), BF16),
            wide, wide, wide, wide,
            narrow, narrow, narrow, narrow,
            listed, listed, listed, listed,
            pltpu.SemaphoreType.DMA((7,)),
        ],
        compiler_params=pltpu.CompilerParams(vmem_limit_bytes=VMEM_LIMIT),
        name="tiles",
    )(order, lens, *arrays)


def scatter_kernel(
    dq_ref, dkv_ref,
    dq_out, dk_out, dv_out,
    own, sib, send2, land2, send1, land1, fin,
    own_sem, sib_send, sib_recv, s2_send, s2_recv, s1_send, s1_recv, f_send, f_recv, q_send, q_recv,
):
    x, z, y, c = place()
    head = 2 * x + z
    enter(x, z, y, c)
    sibling = device(x, z, y, 1 - c)
    up, down = device(x, z, (y + 1) % NY, c), device(x, z, (y + 3) % NY, c)
    planes = [(y + 2) % NY, (y + 1) % NY, (y + 3) % NY, y]
    xs = [(x + dx) % NX for dx in (2, 1, 3, 0)]
    sends = []

    own_copies, sib_copies = {}, {}
    for r, plane in enumerate(planes):
        for n, tx in enumerate(xs):
            at = r * NX + n
            copy = remote(
                dkv_ref.at[plane, 1 - c, tx], sib.at[r, n], sib_send.at[at], sib_recv.at[at], sibling
            )
            copy.start()
            sends.append(copy)
            sib_copies[r, n] = copy
            copy = pltpu.make_async_copy(dkv_ref.at[plane, c, tx], own.at[r, n], own_sem.at[at])
            copy.start()
            own_copies[r, n] = copy

    q_copies = []
    for dx in ORDER:
        for dz in range(2):
            for dc in range(2):
                tx, tz, tc = (x + dx) % NX, (z + dz) % 2, (c + dc) % 2
                src = dq_ref.at[2 * tx + tz, rows_at(tc * ROWS, ROWS), :]
                dst = dq_out.at[:, columns(2 * head + c)]
                at = (dx * 2 + dz) * 2 + dc
                if at == 0:
                    copy = pltpu.make_async_copy(src, dst, q_recv.at[at])
                else:
                    copy = remote(src, dst, q_send.at[at], q_recv.at[at], device(tx, tz, y, tc))
                    sends.append(copy)
                copy.start()
                q_copies.append(copy)

    def arrived(r, n):
        own_copies[r, n].wait()
        sib_copies[r, n].wait_recv()

    def pair_sum(r, n, part):
        return own[r, n, part].astype(F32) + sib[r, n, part].astype(F32)

    copies2 = {}
    for n in range(NX):
        arrived(0, n)
        for part, to in enumerate((up, down)):
            send2[part, n] = pair_sum(0, n, part).astype(BF16)
            at = part * NX + n
            copy = remote(send2.at[part, n], land2.at[part, n], s2_send.at[at], s2_recv.at[at], to)
            copy.start()
            sends.append(copy)
            copies2[part, n] = copy

    copies1 = {}

    def send_on(way, n, part, to):
        at = (way * 2 + part) * NX + n
        copy = remote(send1.at[way, part, n], land1.at[way, part, n], s1_send.at[at], s1_recv.at[at], to)
        copy.start()
        sends.append(copy)
        copies1[way, part, n] = copy

    for n in range(NX):
        for way, to in enumerate((up, down)):
            arrived(1 + way, n)
            part = 1 - way
            send1[way, part, n] = pair_sum(1 + way, n, part).astype(BF16)
            send_on(way, n, part, to)
    for n in range(NX):
        for way, to in enumerate((up, down)):
            part = way
            copies2[part, n].wait_recv()
            send1[way, part, n] = (pair_sum(1 + way, n, part) + land2[part, n].astype(F32)).astype(BF16)
            send_on(way, n, part, to)

    f_copies = []
    for n in range(NX):
        arrived(3, n)
        for part, out in ((0, dk_out), (1, dv_out)):
            for way in range(2):
                copies1[way, part, n].wait_recv()
            total = pair_sum(3, n, part) + land1[0, part, n].astype(F32) + land1[1, part, n].astype(F32)
            fin[part, n] = total.T.astype(BF16)
            for dz in range(2):
                tz = (z + dz) % 2
                src = fin.at[part, n, rows_at(tz * ROWS, ROWS), :]
                dst = out.at[:, columns(head)]
                at = (n * 2 + part) * 2 + dz
                if n == NX - 1 and dz == 0:
                    copy = pltpu.make_async_copy(src, dst, f_recv.at[at])
                    copy.start()
                    f_copies.append((True, copy))
                else:
                    copy = remote(src, dst, f_send.at[at], f_recv.at[at], device(xs[n], tz, y, c))
                    copy.start()
                    sends.append(copy)
                    f_copies.append((False, copy))

    for index, copy in enumerate(q_copies):
        if index == 0:
            copy.wait()
        else:
            copy.wait_recv()
    for local, copy in f_copies:
        if local:
            copy.wait()
        else:
            copy.wait_recv()
    for copy in sends:
        copy.wait_send()


def scatter(dq, dkv):
    hbm = pl.BlockSpec(memory_space=pl.ANY)
    dma = pltpu.SemaphoreType.DMA
    return pl.pallas_call(
        scatter_kernel,
        out_shape=(
            jax.ShapeDtypeStruct((ROWS, 2048), BF16),
            jax.ShapeDtypeStruct((ROWS, 1024), BF16),
            jax.ShapeDtypeStruct((ROWS, 1024), BF16),
        ),
        in_specs=[hbm] * 2,
        out_specs=(hbm,) * 3,
        scratch_shapes=[
            pltpu.VMEM((4, NX, 2, HD, QT), BF16),
            pltpu.VMEM((4, NX, 2, HD, QT), BF16),
            pltpu.VMEM((2, NX, HD, QT), BF16),
            pltpu.VMEM((2, NX, HD, QT), BF16),
            pltpu.VMEM((2, 2, NX, HD, QT), BF16),
            pltpu.VMEM((2, 2, NX, HD, QT), BF16),
            pltpu.VMEM((2, NX, QT, HD), BF16),
            dma((16,)),
            dma((16,)), dma((16,)),
            dma((8,)), dma((8,)),
            dma((16,)), dma((16,)),
            dma((16,)), dma((16,)),
            dma((16,)), dma((16,)),
        ],
        compiler_params=pltpu.CompilerParams(collective_id=1, has_side_effects=True, vmem_limit_bytes=VMEM_LIMIT),
        name="scatter_grads",
    )(dq, dkv)


def body(
    query_states,
    key_states,
    value_states,
    attn_output,
    output_grad,
    logsumexp,
    block_order,
    doc_lengths,
):
    arrays = gather(query_states, key_states, value_states, attn_output, output_grad, logsumexp)
    dq, dkv = tiles(block_order, doc_lengths, *arrays)
    return scatter(dq, dkv.reshape(NY, 2, NX, 2, HD, QT))


def solution(mesh):
    placed = (
        P(("pb", "ka"), "ha"),
        P(("ka", "pb"), "ha"),
        P(("ka", "pb"), "ha"),
        P(("pb", "ka"), "ha"),
        P(("pb", "ka"), "ha"),
        P("ha", ("pb", "ka")),
        P("ha"),
        P("ha"),
    )
    return jax.shard_map(
        body,
        mesh=mesh,
        in_specs=placed,
        out_specs=(P(("pb", "ka"), "ha"), P(("ka", "pb"), "ha"), P(("ka", "pb"), "ha")),
        check_vma=False,
    )
```

time: 105 us -> 101 us (0.962)
  local copies, waits for them, and re-layouts: 11.2 us -> 5.22 us
  Pallas kernels: 93 us -> 95.3 us
    pallas_call x2, Pallas kernels: 50.7 us -> 65.9 us  [the longest x1 35.1 us: gather(): pl.pallas_call(gather_kernel, out_shape=(half, half, turned, turned, spre...]
    pallas_call x1, Pallas kernels: 42.3 us -> 29.4 us  [scatter(): pl.pallas_call(scatter_kernel, out_shape=(jax.ShapeDtypeStruct((ROWS, 204...]
    unnamed x21 -> x3, local copies, waits for them, and re-layouts: 11.2 us -> 5.22 us
where the time goes in v2:
time: 101 us
  Pallas kernels  95.3 us (94%)
  local copies, waits for them, and re-layouts  5.22 us (5%)
    pallas_call x1, Pallas kernels, gather(): pl.pallas_call(gather_kernel, out_shape=(half, half, turned, turned, spre...  35.1 us
    pallas_call x1, Pallas kernels, tiles(): pl.pallas_call(tile_kernel, out_shape=(jax.ShapeDtypeStruct((8, QT, HD),...  30.8 us
    pallas_call x1, Pallas kernels, scatter(): pl.pallas_call(scatter_kernel, out_shape=(jax.ShapeDtypeStruct((ROWS, 204...  29.4 us
    unnamed x3, local copies, waits for them, and re-layouts  5.22 us

profile of v2, /device:TPU:1, one launch (start us, length us, event | category | flops | bytes accessed | tf_op | source)
XLA Modules:
  0.0 101.2 jit_solution(6185373999583820099)
XLA Ops:
  0.6 35.1 %gather_heads.1 = (bf16[8,256,128]{2,1,0:T(8,128)(2,1)}, bf16[8,256,128]{2,1,0:T(8,128)(2,1)}, bf16[8,128,256]{2,1,0:T(8,128)(2,1)}, bf16[8,128,256]{2,1,0:T(8,1...) custom-call(bf16[128,2048]{1,0:T(8,128)(2,1)} %q_ref.1, ...), custom_call_target="tpu_custom_call" | custom-call | tf_op jit(solution)/shard_map/gather_heads/pallas_call | solution.py:221
  35.7 30.8 %tiles.1 = (bf16[8,256,128]{2,1,0:T(8,128)(2,1)}, bf16[32,2,128,256]{3,2,1,0:T(8,128)(2,1)}) custom-call(s32[16]{0:T(128)} %order_ref.1, s32[4]{0:T(128)} %lens_ref.1, bf16[8,256,128]{2,1,0:T(8,128)(2,1)} %get-tuple-element.12.qh_ref, bf16[8,256,128]{2,1,0:T(8,128)(2,1)} %get-tuple-element.13.gh_ref, bf16[8,128,256]{2,1,0:T(8,128)(2,1)} %get-tuple-element.14.qt_ref, ...), custom_call_target="tpu_custom_call" | custom-call | tf_op jit(solution)/shard_map/tiles/pallas_call | solution.py:402
  66.5 29.4 %scatter_grads.1 = (bf16[128,2048]{1,0:T(8,128)(2,1)}, bf16[128,1024]{1,0:T(8,128)(2,1)}, bf16[128,1024]{1,0:T(8,128)(2,1)}) custom-call(bf16[8,256,128]{2,1,0:T(8,128)(2,1)} %get-tuple-element.19.dq_ref, bf16[4,2,4,2,128,256]{5,4,3,2,1,0:T(8,128)(2,1)} %bitcast.1), custom_call_target="tpu_custom_call" | custom-call | tf_op jit(solution)/shard_map/scatter_grads/pallas_call | solution.py:558
  96.0 1.9 %copy.14 = bf16[128,2048]{1,0:T(8,128)(2,1)} copy(bf16[128,2048]{1,0:T(8,128)(2,1)} %get-tuple-element.24) | data formatting | bytes 1048576
  97.8 1.7 %copy.15 = bf16[128,1024]{1,0:T(8,128)(2,1)} copy(bf16[128,1024]{1,0:T(8,128)(2,1)} %get-tuple-element.25) | data formatting | bytes 524288
  99.5 1.7 %copy.16 = bf16[128,1024]{1,0:T(8,128)(2,1)} copy(bf16[128,1024]{1,0:T(8,128)(2,1)} %get-tuple-element.26) | data formatting | bytes 524288

commit v3 on v2

v3 whole, which is shorter than its diff:
```python
from functools import partial
import math

import jax
import jax.numpy as jnp
from jax import lax
from jax.experimental import pallas as pl
from jax.experimental.pallas import tpu as pltpu
from jax.sharding import PartitionSpec as P

HD = 128
BLK = 512
ROWS = 128
NX, NY = 4, 4
VMEM_LIMIT = 60 << 20
BF16 = jnp.bfloat16
F32 = jnp.float32

softcap = 50.0
score_scale = 144.0 ** (-0.5)
log2e = math.log2(math.e)

ORDER = (0, 1, 3, 2)
CHUNKS = ((0, 0), (0, 1), (1, 0), (3, 0), (1, 1), (3, 1), (2, 0), (2, 1))
QT = 256
KT = 256
STEP = 32


def place():
    pb, ka = lax.axis_index("pb"), lax.axis_index("ka")
    return pb // 2, pb % 2, ka // 2, ka % 2


def device(x, z, y, c):
    return {"pb": 2 * x + z, "ka": 2 * y + c}


def remote(src, dst, send, recv, to):
    return pltpu.make_async_remote_copy(
        src_ref=src,
        dst_ref=dst,
        send_sem=send,
        recv_sem=recv,
        device_id=to,
        device_id_type=pl.DeviceIdType.MESH,
    )


def enter(x, z, y, c):
    barrier = pltpu.get_barrier_semaphore()
    for dx in range(NX):
        for dz in range(2):
            for dc in range(2):
                if (dx, dz, dc) != (0, 0, 0):
                    to = device((x + dx) % NX, (z + dz) % 2, y, (c + dc) % 2)
                    pl.semaphore_signal(barrier, inc=1, device_id=to, device_id_type=pl.DeviceIdType.MESH)
    for dy in (1, 3):
        to = device(x, z, (y + dy) % NY, c)
        pl.semaphore_signal(barrier, inc=1, device_id=to, device_id_type=pl.DeviceIdType.MESH)
    pl.semaphore_wait(barrier, 17)


def columns(head, count=1):
    return pl.ds(pl.multiple_of(head * HD, HD), count * HD)


def rows_at(start, count):
    return pl.ds(pl.multiple_of(start, ROWS), count)


def gather_kernel(
    q_ref, k_ref, v_ref, o_ref, g_ref, lse_ref,
    q2_ref, g2_ref, qt_ref, gt_ref, lb_ref, db_ref, kv_ref,
    o_v, g_v, aux_v, qh_v, gh_v, auxh_v, q2_v, g2_v, qt_v, gt_v, lb_v, db_v,
    load_sem, kv_send, kv_recv, y_send, y_recv, y2_send, y2_recv, q_send, q_recv, s_send, s_recv,
    a_send, a_recv, out_sem,
):
    x, z, y, c = place()
    loads = [
        pltpu.make_async_copy(o_ref, o_v, load_sem.at[0]),
        pltpu.make_async_copy(g_ref, g_v, load_sem.at[1]),
    ]
    for load in loads:
        load.start()
    enter(x, z, y, c)

    sibling = device(x, z, y, 1 - c)
    up, down = device(x, z, (y + 1) % NY, c), device(x, z, (y + 3) % NY, c)
    sends = []

    def send(src, dst, send_sem, recv_sem, to):
        copy = remote(src, dst, send_sem, recv_sem, to)
        copy.start()
        sends.append(copy)
        return copy

    def keep(src, dst, sem):
        copy = pltpu.make_async_copy(src, dst, sem)
        copy.start()
        return copy

    kv_copies = {}
    for dx in ORDER:
        for dz in range(2):
            tx, tz = (x + dx) % NX, (z + dz) % 2
            for part, ref in enumerate((k_ref, v_ref)):
                src = ref.at[:, columns(2 * tx + tz)]
                dst = kv_ref.at[y, c, x // 2, rows_at(z * ROWS, ROWS), pl.ds(part * HD, HD)]
                at = (dx * 2 + dz) * 2 + part
                if at < 2:
                    kv_copies[dx, dz, part] = keep(src, dst, kv_recv.at[at])
                else:
                    to = device(tx, tz, y, (c + dx) % 2)
                    kv_copies[dx, dz, part] = send(src, dst, kv_send.at[at], kv_recv.at[at], to)

    def block(plane, dx):
        return plane, (c + dx) % 2, ((x + NX - dx) % NX) // 2

    first, q_copies = {}, {}
    for dx in ORDER:
        for dz in range(2):
            for part in range(2):
                copy = kv_copies[dx, dz, part]
                if dx == 0 and dz == 0:
                    copy.wait()
                else:
                    copy.wait_recv()
        rows = kv_ref.at[block(y, dx)]
        for way, to in ((0, up), (1, down)):
            at = way * NX + dx
            first[way, dx] = send(rows, rows, y_send.at[at], y_recv.at[at], to)
        for j, (jx, jz) in enumerate(CHUNKS):
            if jx != dx:
                continue
            tx, tz = (x + jx) % NX, (z + jz) % 2
            for kind, (ref, out) in enumerate(((q_ref, qh_v), (g_ref, gh_v))):
                src = ref.at[:, columns(2 * (2 * tx + tz), 2)]
                dst = out.at[2 * x + z, rows_at(c * ROWS, ROWS), :]
                at = 2 * j + kind
                if j == 0:
                    q_copies[j, kind] = keep(src, dst, q_recv.at[at])
                else:
                    q_copies[j, kind] = send(src, dst, q_send.at[at], q_recv.at[at], device(tx, tz, y, c))

    for load in loads:
        load.wait()
    for h in range(8):
        rows = [lse_ref[2 * h : 2 * h + 2, :] * log2e]
        for n in range(2):
            cols = pl.ds((2 * h + n) * HD, HD)
            prod = g_v[:, cols].astype(F32) * o_v[:, cols].astype(F32)
            rows.append(jnp.sum(prod.T, axis=0, keepdims=True))
        aux_v[h] = jnp.concatenate(rows + [jnp.zeros((4, ROWS), F32)], axis=0)
    a_copies = []
    for j, (dx, dz) in enumerate(CHUNKS):
        tx, tz = (x + dx) % NX, (z + dz) % 2
        for dc in range(2):
            src, dst, at = aux_v.at[2 * tx + tz], auxh_v.at[2 * (2 * x + z) + c], 2 * j + dc
            if at == 0:
                a_copies.append(keep(src, dst, a_recv.at[at]))
            else:
                a_copies.append(send(src, dst, a_send.at[at], a_recv.at[at], device(tx, tz, y, (c + dc) % 2)))

    second = {}
    for dx in ORDER:
        for way, (plane, to) in enumerate((((y + 3) % NY, up), ((y + 1) % NY, down))):
            first[way, dx].wait_recv()
            at = way * NX + dx
            half = kv_ref.at[block(plane, dx)].at[:, pl.ds(way * HD, HD)]
            second[way, dx] = send(half, half, y2_send.at[at], y2_recv.at[at], to)

    for n, copy in enumerate(a_copies):
        if n == 0:
            copy.wait()
        else:
            copy.wait_recv()
    outs, passed = [], {}
    for j in range(len(CHUNKS) + 1):
        if j < len(CHUNKS):
            dx, dz = CHUNKS[j]
            i = 2 * ((x + NX - dx) % NX) + (z + 2 - dz) % 2
            for kind, out in enumerate((qh_v, gh_v)):
                if j == 0:
                    q_copies[j, kind].wait()
                else:
                    q_copies[j, kind].wait_recv()
                rows = out.at[i, rows_at(c * ROWS, ROWS), :]
                at = 2 * j + kind
                passed[j, kind] = send(rows, rows, s_send.at[at], s_recv.at[at], sibling)
        if j > 0:
            dx, dz = CHUNKS[j - 1]
            i = 2 * ((x + NX - dx) % NX) + (z + 2 - dz) % 2
            for kind in range(2):
                passed[j - 1, kind].wait_recv()
            for h in range(2):
                rows = slice(h * QT, (h + 1) * QT)
                for whole, split, turned in ((qh_v, q2_v, qt_v), (gh_v, g2_v, gt_v)):
                    part = whole[i, :, h * HD : (h + 1) * HD]
                    split[i, rows, :] = part
                    turned[i, :, rows] = part.T
            for n in range(2):
                spread = auxh_v[2 * i + n].T
                for h in range(2):
                    rows = slice(h * QT + n * ROWS, h * QT + (n + 1) * ROWS)
                    lb_v[i, rows, :] = jnp.broadcast_to(spread[:, h : h + 1], (ROWS, HD))
                    db_v[i, rows, :] = jnp.broadcast_to(spread[:, 2 + h : 3 + h], (ROWS, HD))
            for n, (src, dst) in enumerate(
                ((q2_v, q2_ref), (g2_v, g2_ref), (qt_v, qt_ref), (gt_v, gt_ref), (lb_v, lb_ref), (db_v, db_ref))
            ):
                outs.append(keep(src.at[i], dst.at[i], out_sem.at[j - 1, n]))

    for copy in second.values():
        copy.wait_recv()
    for copy in sends:
        copy.wait_send()
    for copy in outs:
        copy.wait()


def gather(q, k, v, o, g, lse):
    hbm = pl.BlockSpec(memory_space=pl.ANY)
    dma = pltpu.SemaphoreType.DMA
    split = (8, 2 * QT, HD)
    turned = (8, HD, 2 * QT)
    return pl.pallas_call(
        gather_kernel,
        out_shape=tuple(
            jax.ShapeDtypeStruct(shape, kind)
            for shape, kind in (
                (split, BF16), (split, BF16), (turned, BF16), (turned, BF16), (split, F32), (split, F32),
                ((NY, 2, 2, KT, 2 * HD), BF16),
            )
        ),
        in_specs=[hbm] * 5 + [pl.BlockSpec(memory_space=pltpu.VMEM)],
        out_specs=(hbm,) * 7,
        scratch_shapes=[
            pltpu.VMEM((ROWS, 2048), BF16),
            pltpu.VMEM((ROWS, 2048), BF16),
            pltpu.VMEM((8, 8, ROWS), F32),
            pltpu.VMEM((8, QT, 2 * HD), BF16),
            pltpu.VMEM((8, QT, 2 * HD), BF16),
            pltpu.VMEM((16, 8, ROWS), F32),
            pltpu.VMEM(split, BF16),
            pltpu.VMEM(split, BF16),
            pltpu.VMEM(turned, BF16),
            pltpu.VMEM(turned, BF16),
            pltpu.VMEM(split, F32),
            pltpu.VMEM(split, F32),
            dma((2,)),
            dma((16,)), dma((16,)),
            dma((8,)), dma((8,)),
            dma((8,)), dma((8,)),
            dma((16,)), dma((16,)),
            dma((16,)), dma((16,)),
            dma((16,)), dma((16,)),
            dma((8, 6)),
        ],
        compiler_params=pltpu.CompilerParams(collective_id=0, has_side_effects=True, vmem_limit_bytes=VMEM_LIMIT),
        name="gather_heads",
    )(q, k, v, o, g, lse)


def nt(a, b):
    return lax.dot_general(a, b, (((1,), (1,)), ((), ())), preferred_element_type=F32)


def nn(a, b):
    return jnp.dot(a, b, preferred_element_type=F32)


def tile_kernel(part, *refs):
    if part == 0:
        (order_ref, lens_ref, q2_ref, g2_ref, qt_ref, gt_ref, lb_ref, db_ref, kv_ref, dq_ref, *dkv_refs), refs = (
            refs[:14], refs[14:],
        )
    else:
        (order_ref, lens_ref, q2_ref, g2_ref, qt_ref, gt_ref, lb_ref, db_ref, kv_ref, old_ref, dq_ref, *dkv_refs), refs = (
            refs[:12], refs[12:],
        )
    (
        q_v, g_v, qt_v, gt_v, lb_v, db_v, kv_v, acc_q, acc_k, acc_v, dq_v, dkv_v,
        s_a, s_b, dp_a, dp_b, p_a, p_b, ds_a, ds_b, tile_q, tile_k, tile_at, tile_cut, sems,
    ) = refs
    x, z, y, c = place()
    core = (c + part) % 2
    loads = [
        pltpu.make_async_copy(src, dst, sems.at[n])
        for n, (src, dst) in enumerate(
            (
                (kv_ref.at[:, core], kv_v), (q2_ref, q_v), (g2_ref, g_v),
                (lb_ref, lb_v), (db_ref, db_v), (qt_ref, qt_v), (gt_ref, gt_v),
            )
        )
    ]
    if part == 1:
        loads.append(pltpu.make_async_copy(old_ref, acc_q, sems.at[7]))
    for load in loads:
        load.start()
    starts = [lens_ref[0], lens_ref[0] + lens_ref[1], lens_ref[0] + lens_ref[1] + lens_ref[2]]

    def low_of(p):
        low = jnp.zeros_like(p)
        for start in starts:
            low = jnp.where(p >= start, start, low)
        return low

    base = [order_ref[2 * i + y // 2] * BLK + (y % 2) * QT for i in range(8)]
    first_low = [low_of(base[i]) for i in range(8)]
    last_low = [low_of(base[i] + (QT - 1)) for i in range(8)]

    def list_slot(slot, count):
        stored = 4 * (slot // 2) + 2 * core + slot % 2
        key = order_ref[stored] * BLK + ((x + c + core) % 2) * KT
        for i in range(8):
            needed = jnp.logical_and(key < base[i] + QT, key + KT > first_low[i])
            whole = jnp.logical_and(key + KT <= base[i] + 1, key >= last_low[i])
            tile_q[count] = i
            tile_k[count] = slot
            tile_at[count] = key - base[i]
            tile_cut[count] = jnp.where(whole, 0, 1)
            count = count + needed.astype(jnp.int32)
        return count

    count = lax.fori_loop(0, 8, list_slot, 0)
    for n in range(2):
        tile_q[count + n] = 0
        tile_k[count + n] = 0
        tile_at[count + n] = 1 << 20
        tile_cut[count + n] = 1
    pairs = (count + 1) // 2
    last = jnp.maximum(2 * pairs - 1, 1)

    for slot in range(8):
        acc_k[slot] = jnp.zeros((HD, KT), F32)
        acc_v[slot] = jnp.zeros((HD, KT), F32)
    if part == 0:

        def clear(i, _):
            acc_q[i] = jnp.zeros((2 * QT, HD), F32)
            return 0

        lax.fori_loop(0, 8, clear, 0)

    def keys(t):
        return kv_v[tile_k[t] // 2, tile_k[t] % 2, :, 0:HD]

    def values(t):
        return kv_v[tile_k[t] // 2, tile_k[t] % 2, :, HD : 2 * HD]

    def scores(t, s_ref, dp_ref):
        i = tile_q[t]

        def piece(out, left, right, h):
            rows = slice(h * QT, (h + 1) * QT)
            out[rows, :] = nt(left[i, rows, :], right(t))

        return [
            partial(piece, out, left, right, h)
            for out, left, right in ((s_ref, q_v, keys), (dp_ref, g_v, values))
            for h in range(2)
        ]

    def weigh(t, s_ref, dp_ref, p_ref, ds_ref, cut):
        i, at = tile_q[t], tile_at[t]
        if cut:
            query_base = order_ref[2 * i + y // 2] * BLK + (y % 2) * QT
        step = STEP

        def piece(r):
            lse = lb_v[i, r : r + step, :]
            delta = db_v[i, r : r + step, :]
            lse = jnp.concatenate([lse] * (KT // HD), axis=1)
            delta = jnp.concatenate([delta] * (KT // HD), axis=1)
            th = jnp.tanh(s_ref[r : r + step, :] * (score_scale / softcap))
            p = jnp.exp2(th * (softcap * log2e) - lse)
            if cut:
                row = lax.broadcasted_iota(jnp.int32, (step, HD), 0) + r % QT
                low = low_of(row + query_base) - query_base
                row = jnp.concatenate([row] * (KT // HD), axis=1)
                low = jnp.concatenate([low] * (KT // HD), axis=1)
                key = lax.broadcasted_iota(jnp.int32, (step, KT), 1) + at
                p = jnp.where((key <= row) & (key >= low), p, 0.0)
            ds = p * (dp_ref[r : r + step, :] - delta) * ((1.0 - th * th) * score_scale)
            p_ref[r : r + step, :] = p.astype(BF16)
            ds_ref[r : r + step, :] = ds.astype(BF16)

        return [partial(piece, r) for r in range(0, 2 * QT, step)]

    def gradients(t, p_ref, ds_ref):
        i, slot = tile_q[t], tile_k[t]

        def key_piece(out, left, right):
            out[slot] += nn(left[i], right[...])

        def query_piece(h):
            rows = slice(h * QT, (h + 1) * QT)
            acc_q[i, rows, :] += nn(ds_ref[rows, :], keys(t))

        return [
            partial(key_piece, acc_v, gt_v, p_ref),
            partial(key_piece, acc_k, qt_v, ds_ref),
            partial(query_piece, 0),
            partial(query_piece, 1),
        ]

    def run(*lists):
        marked = [((n + 0.5) / len(pieces), m, piece) for m, pieces in enumerate(lists) for n, piece in enumerate(pieces)]
        for _, _, piece in sorted(marked, key=lambda entry: entry[:2]):
            piece()

    buffers = ((s_a, dp_a, p_a, ds_a), (s_b, dp_b, p_b, ds_b))

    def step(t, parity):
        s0, dp0, p0, ds0 = buffers[parity]
        s1, dp1, p1, ds1 = buffers[1 - parity]
        middle = jnp.minimum(t + 1, last)

        def whole_step(cut):
            run(
                scores(jnp.minimum(t + 2, last), s0, dp0) + gradients(t, p0, ds0),
                weigh(middle, s1, dp1, p1, ds1, cut),
            )

        pl.when(tile_cut[middle] == 0)(lambda: whole_step(False))
        pl.when(tile_cut[middle] != 0)(lambda: whole_step(True))

    for load in loads[:3]:
        load.wait()
    run(scores(0, s_a, dp_a))
    for load in loads[3:5]:
        load.wait()
    run(scores(1, s_b, dp_b), weigh(0, s_a, dp_a, p_a, ds_a, True))
    for load in loads[5:]:
        load.wait()

    def pair(n, _):
        step(2 * n, 0)
        step(2 * n + 1, 1)
        return 0

    lax.fori_loop(0, pairs, pair, 0)

    outs = []
    if part == 0:
        outs.append(pltpu.make_async_copy(acc_q, dq_ref, sems.at[0]))
        outs[0].start()
    for d in range(NY):
        plane = (y + d) % NY
        for h in range(2):
            dkv_v[d, h, 0] = acc_k[2 * plane + h].astype(BF16)
            dkv_v[d, h, 1] = acc_v[2 * plane + h].astype(BF16)
        out = dkv_refs[d] if part == 0 else dkv_refs[0].at[d]
        outs.append(pltpu.make_async_copy(dkv_v.at[d], out, sems.at[1 + d]))
        outs[-1].start()
    if part == 1:

        def narrow(i, _):
            for h in range(2):
                dq_v[h, i] = acc_q[i, h * QT : (h + 1) * QT, :].astype(BF16)
            return 0

        lax.fori_loop(0, 8, narrow, 0)
        outs.append(pltpu.make_async_copy(dq_v, dq_ref, sems.at[0]))
        outs[-1].start()
    for out in outs:
        out.wait()


def tiles(part, order, lens, arrays, old=()):
    smem = pl.BlockSpec(memory_space=pltpu.SMEM)
    hbm = pl.BlockSpec(memory_space=pl.ANY)
    split = (8, 2 * QT, HD)
    turned = (8, HD, 2 * QT)
    wide = pltpu.VMEM((2 * QT, KT), F32)
    narrow = pltpu.VMEM((2 * QT, KT), BF16)
    listed = pltpu.SMEM((72,), jnp.int32)
    sums = (2, 2, HD, KT)
    if part == 0:
        out_shape = (jax.ShapeDtypeStruct(split, F32),) + (jax.ShapeDtypeStruct(sums, BF16),) * NY
    else:
        out_shape = (jax.ShapeDtypeStruct((2, 8, QT, HD), BF16), jax.ShapeDtypeStruct((NY,) + sums, BF16))
    return pl.pallas_call(
        partial(tile_kernel, part),
        out_shape=out_shape,
        in_specs=[smem, smem] + [hbm] * (len(arrays) + len(old)),
        out_specs=(hbm,) * len(out_shape),
        scratch_shapes=[
            pltpu.VMEM(split, BF16),
            pltpu.VMEM(split, BF16),
            pltpu.VMEM(turned, BF16),
            pltpu.VMEM(turned, BF16),
            pltpu.VMEM(split, F32),
            pltpu.VMEM(split, F32),
            pltpu.VMEM((NY, 2, KT, 2 * HD), BF16),
            pltpu.VMEM(split, F32),
            pltpu.VMEM((8, HD, KT), F32),
            pltpu.VMEM((8, HD, KT), F32),
            pltpu.VMEM((2, 8, QT, HD), BF16),
            pltpu.VMEM((NY,) + sums, BF16),
            wide, wide, wide, wide,
            narrow, narrow, narrow, narrow,
            listed, listed, listed, listed,
            pltpu.SemaphoreType.DMA((8,)),
        ],
        compiler_params=pltpu.CompilerParams(vmem_limit_bytes=VMEM_LIMIT),
        cost_estimate=pl.CostEstimate(flops=6 * 10**9, bytes_accessed=16 << 20, transcendentals=4 << 20),
        name="tiles_a" if part == 0 else "tiles_b",
    )(order, lens, *arrays, *old)


def scatter_kernel(
    dq_ref, dkv_ref, a0_ref, a1_ref, a2_ref, a3_ref,
    dq_out, dk_out, dv_out,
    own, near, land2, send1, land1, fin, mine, theirs, dq_v,
    load_sem, near_sem, mine_sem, sib_send, sib_recv, s2_send, s2_recv, s1_send, s1_recv, f_send, f_recv, q_send, q_recv,
):
    x, z, y, c = place()
    head = 2 * x + z
    loads = [pltpu.make_async_copy(dkv_ref.at[d], own.at[d], load_sem.at[d]) for d in range(NY)]
    near_loads = [
        pltpu.make_async_copy(ref, near.at[n], near_sem.at[n]) for n, ref in enumerate((a0_ref, a1_ref, a2_ref, a3_ref))
    ]
    mine_load = pltpu.make_async_copy(dq_ref.at[c], mine, mine_sem)
    for load in [mine_load] + loads + near_loads:
        load.start()
    enter(x, z, y, c)
    sibling = device(x, z, y, 1 - c)
    ways = (device(x, z, (y + 1) % NY, c), device(x, z, (y + 3) % NY, c))
    sends = []

    def send(src, dst, send_sem, recv_sem, to):
        copy = remote(src, dst, send_sem, recv_sem, to)
        copy.start()
        sends.append(copy)
        return copy

    copies2, copies1 = {}, {}
    for h in range(2):
        for part, to in enumerate(ways):
            at = part * 2 + h
            copies2[part, h] = send(dkv_ref.at[2, h, part], land2.at[part, h], s2_send.at[at], s2_recv.at[at], to)
    sib_copy = send(dq_ref.at[1 - c], theirs, sib_send, sib_recv, sibling)
    for h in range(2):
        for way, to in enumerate(ways):
            part = 1 - way
            at = (way * 2 + part) * 2 + h
            copies1[way, part, h] = send(
                dkv_ref.at[1 + 2 * way, h, part], land1.at[way, part, h], s1_send.at[at], s1_recv.at[at], to
            )

    mine_load.wait()
    sib_copy.wait_recv()
    q_copies = []
    for dx, dz in CHUNKS:
        tx, tz = (x + dx) % NX, (z + dz) % 2
        i = 2 * tx + tz
        dq_v[i] = (mine[i].astype(F32) + theirs[i].astype(F32)).astype(BF16)
        for dc in range(2):
            tc = (c + dc) % 2
            src = dq_v.at[i, rows_at(tc * ROWS, ROWS), :]
            dst = dq_out.at[:, columns(2 * head + c)]
            at = (dx * 2 + dz) * 2 + dc
            if at == 0:
                copy = pltpu.make_async_copy(src, dst, q_recv.at[at])
                copy.start()
                q_copies.append((True, copy))
            else:
                q_copies.append((False, send(src, dst, q_send.at[at], q_recv.at[at], device(tx, tz, y, tc))))

    for load in loads:
        load.wait()
    for h in range(2):
        for way, to in enumerate(ways):
            part = way
            copies2[part, h].wait_recv()
            total = own[1 + 2 * way, h, part].astype(F32) + land2[part, h].astype(F32)
            send1[way, h] = total.astype(BF16)
            at = (way * 2 + part) * 2 + h
            copies1[way, part, h] = send(
                send1.at[way, h], land1.at[way, part, h], s1_send.at[at], s1_recv.at[at], to
            )

    f_copies = []

    def final(dx, part, out, total):
        fin[dx, part] = total.T.astype(BF16)
        for dz in range(2):
            tz = (z + dz) % 2
            src = fin.at[dx, part, rows_at(tz * ROWS, ROWS), :]
            dst = out.at[:, columns(head)]
            at = (dx * 2 + part) * 2 + dz
            if dx == 0 and dz == 0:
                copy = pltpu.make_async_copy(src, dst, f_recv.at[at])
                copy.start()
                f_copies.append((True, copy))
            else:
                to = device((x + dx) % NX, tz, y, (c + dx) % 2)
                f_copies.append((False, send(src, dst, f_send.at[at], f_recv.at[at], to)))

    for load in near_loads:
        load.wait()
    for dx in (2, 0):
        h = ((x + dx) % NX) // 2
        for part, out in ((0, dk_out), (1, dv_out)):
            total = near[0, h, part].astype(F32)
            for n in range(1, 4):
                total = total + near[n, h, part].astype(F32)
            final(dx, part, out, total)
    for h in range(2):
        for way in range(2):
            for part in range(2):
                copies1[way, part, h].wait_recv()
    for dx in (1, 3):
        h = ((x + dx) % NX) // 2
        for part, out in ((0, dk_out), (1, dv_out)):
            total = own[0, h, part].astype(F32) + land1[0, part, h].astype(F32) + land1[1, part, h].astype(F32)
            final(dx, part, out, total)

    for local, copy in q_copies + f_copies:
        if local:
            copy.wait()
        else:
            copy.wait_recv()
    for copy in sends:
        copy.wait_send()


def scatter(*arrays):
    hbm = pl.BlockSpec(memory_space=pl.ANY)
    dma = pltpu.SemaphoreType.DMA
    return pl.pallas_call(
        scatter_kernel,
        out_shape=(
            jax.ShapeDtypeStruct((ROWS, 2048), BF16),
            jax.ShapeDtypeStruct((ROWS, 1024), BF16),
            jax.ShapeDtypeStruct((ROWS, 1024), BF16),
        ),
        in_specs=[hbm] * len(arrays),
        out_specs=(hbm,) * 3,
        scratch_shapes=[
            pltpu.VMEM((NY, 2, 2, HD, KT), BF16),
            pltpu.VMEM((NY, 2, 2, HD, KT), BF16),
            pltpu.VMEM((2, 2, HD, KT), BF16),
            pltpu.VMEM((2, 2, HD, KT), BF16),
            pltpu.VMEM((2, 2, 2, HD, KT), BF16),
            pltpu.VMEM((NX, 2, KT, HD), BF16),
            pltpu.VMEM((8, QT, HD), BF16),
            pltpu.VMEM((8, QT, HD), BF16),
            pltpu.VMEM((8, QT, HD), BF16),
            dma((NY,)), dma((NY,)), dma,
            dma, dma,
            dma((4,)), dma((4,)),
            dma((8,)), dma((8,)),
            dma((16,)), dma((16,)),
            dma((16,)), dma((16,)),
        ],
        compiler_params=pltpu.CompilerParams(collective_id=1, has_side_effects=True, vmem_limit_bytes=VMEM_LIMIT),
        name="scatter_grads",
    )(*arrays)


def store_kernel(*refs):
    count = len(refs) // 2
    sems = refs[-1]
    copies = [pltpu.make_async_copy(refs[n], refs[count + n], sems.at[n]) for n in range(count)]
    for copy in copies:
        copy.start()
    for copy in copies:
        copy.wait()


def store(*arrays):
    hbm = pl.BlockSpec(memory_space=pl.ANY)
    return pl.pallas_call(
        store_kernel,
        out_shape=tuple(jax.ShapeDtypeStruct(array.shape, array.dtype) for array in arrays),
        in_specs=[hbm] * len(arrays),
        out_specs=(hbm,) * len(arrays),
        scratch_shapes=[pltpu.SemaphoreType.DMA((len(arrays),))],
        compiler_params=pltpu.CompilerParams(vmem_limit_bytes=VMEM_LIMIT),
        name="store_grads",
    )(*arrays)


def body(
    query_states,
    key_states,
    value_states,
    attn_output,
    output_grad,
    logsumexp,
    block_order,
    doc_lengths,
):
    arrays = gather(query_states, key_states, value_states, attn_output, output_grad, logsumexp)
    dq, *near = tiles(0, block_order, doc_lengths, arrays)
    for d in (2, 1, 3):
        pairs = [(2 * plane + core, 2 * ((plane + d) % NY) + core) for plane in range(NY) for core in range(2)]
        near[d] = lax.ppermute(near[d], "ka", pairs)
    dq, dkv = tiles(1, block_order, doc_lengths, arrays, (dq,))
    return store(*scatter(dq, dkv, *near))


def solution(mesh):
    placed = (
        P(("pb", "ka"), "ha"),
        P(("ka", "pb"), "ha"),
        P(("ka", "pb"), "ha"),
        P(("pb", "ka"), "ha"),
        P(("pb", "ka"), "ha"),
        P("ha", ("pb", "ka")),
        P("ha"),
        P("ha"),
    )
    return jax.shard_map(
        body,
        mesh=mesh,
        in_specs=placed,
        out_specs=(P(("pb", "ka"), "ha"), P(("ka", "pb"), "ha"), P(("ka", "pb"), "ha")),
        check_vma=False,
    )
```

time: 101 us -> 129 us (1.28)
  Pallas kernels: 95.3 us -> 122 us
  starting transfers between devices: 0 us -> 5.42 us
  local copies, waits for them, and re-layouts: 5.22 us -> 0.83 us
    pallas_call x2 -> x4, Pallas kernels: 65.9 us -> 99.4 us  [the longest x1 37.3 us: gather(): pl.pallas_call(gather_kernel, out_shape=tuple((jax.ShapeDtypeStruct(shape...]
    pallas_call x1, Pallas kernels: 29.4 us -> 22.2 us  [scatter(): pl.pallas_call(scatter_kernel, out_shape=(jax.ShapeDtypeStruct((ROWS, 204...]
    ppermute x0 -> x3, starting transfers between devices: none -> 5.42 us  [body(): near[d] = lax.ppermute(near[d], 'ka', pairs)]
    unnamed x3 -> x6, local copies, waits for them, and re-layouts: 5.22 us -> 0.83 us
  transfers between devices with their start and end apart: 0 -> 3, of which waited for: 0 -> 0; matrix products, arithmetic and copies ran while one was open for 0% -> 0% of each run, Pallas kernels for 0% -> 11%
where the time goes in v3:
time: 129 us
  Pallas kernels  122 us (95%)
  starting transfers between devices  5.42 us (4%)
    pallas_call x1, Pallas kernels, gather(): pl.pallas_call(gather_kernel, out_shape=tuple((jax.ShapeDtypeStruct(shape...  37.3 us
    pallas_call x1, Pallas kernels, store(): pl.pallas_call(store_kernel, out_shape=tuple((jax.ShapeDtypeStruct(array....  32.9 us
    pallas_call x2, Pallas kernels, tiles(): pl.pallas_call(partial(tile_kernel, part), out_shape=out_shape, in_specs=...  29.2 us
    pallas_call x1, Pallas kernels, scatter(): pl.pallas_call(scatter_kernel, out_shape=(jax.ShapeDtypeStruct((ROWS, 204...  22.2 us
    ppermute x3, starting transfers between devices, body(): near[d] = lax.ppermute(near[d], 'ka', pairs)  5.42 us
  transfers between devices with their start and end apart: 3, of which 0 were waited for; matrix products, arithmetic and copies ran while one was open for 0% of the time, Pallas kernels for 11%

profile of v3, /device:TPU:1, one launch (start us, length us, event | category | flops | bytes accessed | tf_op | source)
XLA Modules:
  0.0 128.6 jit_solution(5714986247306274020)
XLA Ops:
  0.6 37.3 %gather_heads.1 = (bf16[8,512,128]{2,1,0:T(8,128)(2,1)}, bf16[8,512,128]{2,1,0:T(8,128)(2,1)}, bf16[8,128,512]{2,1,0:T(8,128)(2,1)}, bf16[8,128,512]{2,1,0:T(8,1...) custom-call(bf16[128,2048]{1,0:T(8,128)(2,1)} %q_ref.1, ...), custom_call_target="tpu_custom_call" | custom-call | tf_op jit(solution)/shard_map/gather_heads/pallas_call | solution.py:226
  38.0 15.5 %tiles_a.1 = (f32[8,512,128]{2,1,0:T(8,128)}, bf16[2,2,128,256]{3,2,1,0:T(8,128)(2,1)}, bf16[2,2,128,256]{3,2,1,0:T(8,128)(2,1)}, bf16[2,2,128,256]{3,2,1,0:T(8,128)(2,1)}, bf16[2,2,128,256]{3,2,1,0:T(8,128)(2,1)}) custom-call(s32[16]{0:T(128)} %refs_0_.3, s32[4]{0:T(128)} %refs_1_.3, bf16[8,512,128]{2,1,0:T(8,128)(2,1)} %get-tuple-element.20.refs_2_, ...), custom_call_target="tpu_custom_call" | custom-call | flops 6000000000 | bytes 16777216 | tf_op jit(solution)/shard_map/tiles_a/pallas_call | solution.py:483
  53.5 0.1 collective-permute-start
  53.6 4.1 %collective-permute-start.1 = (bf16[2,2,128,256]{3,2,1,0:T(8,128)(2,1)}, bf16[2,2,128,256]{3,2,1,0:T(8,128)(2,1)S(1)}, u32[]{:S(2)}, u32[]{:S(2)}) collective-permute-start(bf16[2,2,128,256]{3,2,1,0:T(8,128)(2,1)} %get-tuple-element.32), channel_id=1, source_target_pairs={{0,8},{2,10},{4,12},{6,14},{8,0},{10,2},{12,4},{14,6},{1,9},{3,11}... | collective-permute-start | bytes 786440 | tf_op jit(solution)/shard_map/ppermute | solution.py:700
  57.7 1.2 collective-permute-start.2
  58.9 13.7 %tiles_b.1 = (bf16[2,8,256,128]{3,2,1,0:T(8,128)(2,1)}, bf16[4,2,2,128,256]{4,3,2,1,0:T(8,128)(2,1)}) custom-call(s32[16]{0:T(128)} %refs_0_.3, s32[4]{0:T(128)} %refs_1_.3, bf16[8,512,128]{2,1,0:T(8,128)(2,1)} %get-tuple-element.20.refs_2_, bf16[8,512,128]{2,1,0:T(8,128)(2,1)} %get-tuple-element.21.refs_3_, bf16[8,128,512]{2,1,0:T(8,128)(2,1)} %get-tuple-element.22.refs_4_, ...), custom_call_target="tpu_custom_call" | custom-call | flops 6000000000 | bytes 16777216 | tf_op jit(solution)/shard_map/tiles_b/pallas_call | solution.py:483
  72.6 0.0 collective-permute-done.a1_ref
  72.6 0.0 copy-start
  72.6 0.0 collective-permute-done.1.a2_ref
  72.6 0.0 copy-start.1
  72.7 0.0 collective-permute-done.2.a3_ref
  72.7 0.0 copy-start.2
  72.7 0.7 copy-done
  73.3 0.1 copy-done.1
  73.4 0.1 copy-done.2
  73.5 22.2 %scatter_grads.1 = (bf16[128,2048]{1,0:T(8,128)(2,1)}, bf16[128,1024]{1,0:T(8,128)(2,1)}, bf16[128,1024]{1,0:T(8,128)(2,1)}) custom-call(bf16[2,8,256,128]{3,2,1,0:T(8,128)(2,1)} %get-tuple-element.28.dq_ref, bf16[4,2,2,128,256]{4,3,2,1,0:T(8,128)(2,1)} %get-tuple-element.29.dkv_ref, bf16[2,2,128,256]{3,2,1,0:T(8,128)(2,1)} %get-tuple-element.30.a0_ref, ...), custom_call_target="tpu_custom_call" | custom-call | tf_op jit(solution)/shard_map/scatter_grads/pallas_call | solution.py:632
  95.7 32.9 %store_grads.1 = (bf16[128,2048]{1,0:T(8,128)(2,1)}, bf16[128,1024]{1,0:T(8,128)(2,1)}, bf16[128,1024]{1,0:T(8,128)(2,1)}) custom-call(bf16[128,2048]{1,0:T(8,128)(2,1)} %get-tuple-element.34.refs_0_, bf16[128,1024]{1,0:T(8,128)(2,1)} %get-tuple-element.35.refs_1_, bf16[128,1024]{1,0:T(8,128)(2,1)} %get-tuple-element.36.refs_2_), custom_call_target="tpu_custom_call" | custom-call | tf_op jit(solution)/shard_map/store_grads/pallas_call | solution.py:675
Async XLA Ops:
  53.5 19.1 %collective-permute-start = (bf16[2,2,128,256]{3,2,1,0:T(8,128)(2,1)}, bf16[2,2,128,256]{3,2,1,0:T(8,128)(2,1)S(1)}, u32[]{:S(2)}, u32[]{:S(2)}) collective-permute-start(bf16[2,2,128,256]{3,2,1,0:T(8,128)(2,1)} %get-tuple-element.31), channel_id=1, source_target_pairs={{0,4},{2,6},{4,8},{6,10},{8,12},{10,14},{12,0},{14,2},{1,5},{3,7},... | collective-permute-start | bytes 786440 | tf_op jit(solution)/shard_map/ppermute | solution.py:700
  53.6 19.1 %collective-permute-start.1 = (bf16[2,2,128,256]{3,2,1,0:T(8,128)(2,1)}, bf16[2,2,128,256]{3,2,1,0:T(8,128)(2,1)S(1)}, u32[]{:S(2)}, u32[]{:S(2)}) collective-permute-start(bf16[2,2,128,256]{3,2,1,0:T(8,128)(2,1)} %get-tuple-element.32), channel_id=1, source_target_pairs={{0,8},{2,10},{4,12},{6,14},{8,0},{10,2},{12,4},{14,6},{1,9},{3,11}... | collective-permute-start | bytes 786440 | tf_op jit(solution)/shard_map/ppermute | solution.py:700
  57.7 15.0 %collective-permute-start.2 = (bf16[2,2,128,256]{3,2,1,0:T(8,128)(2,1)}, bf16[2,2,128,256]{3,2,1,0:T(8,128)(2,1)S(1)}, u32[]{:S(2)}, u32[]{:S(2)}) collective-permute-start(bf16[2,2,128,256]{3,2,1,0:T(8,128)(2,1)} %get-tuple-element.33), channel_id=1, source_target_pairs={{0,12},{2,14},{4,0},{6,2},{8,4},{10,6},{12,8},{14,10},{1,13},{3,15... | collective-permute-start | bytes 786440 | tf_op jit(solution)/shard_map/ppermute | solution.py:700
  72.6 0.7 copy-start
  72.6 0.8 copy-start.1
  72.7 0.8 copy-start.2

commit v4 on v3

--- a/solution.py
+++ b/solution.py
@@ -21,7 +21,8 @@
 log2e = math.log2(math.e)
 
 ORDER = (0, 1, 3, 2)
-CHUNKS = ((0, 0), (0, 1), (1, 0), (3, 0), (1, 1), (3, 1), (2, 0), (2, 1))
+CHUNKS = ((0, 0), (2, 1), (2, 0), (1, 1), (3, 1), (0, 1), (1, 0), (3, 0))
+PASS = ((0,), (1,), (2, 3), (4, 5))
 QT = 256
 KT = 256
 STEP = 32
@@ -101,8 +102,7 @@
         return copy
 
     kv_copies = {}
-    for dx in ORDER:
-        for dz in range(2):
+    for dx, dz in ((0, 0), (0, 1), (1, 0), (3, 0), (1, 1), (3, 1), (2, 0), (2, 1)):
             tx, tz = (x + dx) % NX, (z + dz) % 2
             for part, ref in enumerate((k_ref, v_ref)):
                 src = ref.at[:, columns(2 * tx + tz)]
@@ -131,7 +131,7 @@
             at = way * NX + dx
             first[way, dx] = send(rows, rows, y_send.at[at], y_recv.at[at], to)
         for j, (jx, jz) in enumerate(CHUNKS):
-            if jx != dx:
+            if dx != 0:
                 continue
             tx, tz = (x + jx) % NX, (z + jz) % 2
             for kind, (ref, out) in enumerate(((q_ref, qh_v), (g_ref, gh_v))):
@@ -145,13 +145,18 @@
 
     for load in loads:
         load.wait()
+    delta = jnp.zeros((16, ROWS), F32)
+    for h in range(16):
+        cols = pl.ds(h * HD, HD)
+        prod = g_v[:, cols].astype(F32) * o_v[:, cols].astype(F32)
+        high = prod.astype(BF16)
+        low = (prod - high.astype(F32)).astype(BF16)
+        pick = jnp.where(lax.broadcasted_iota(jnp.int32, (16, HD), 0) == h, 1.0, 0.0).astype(BF16)
+        delta = delta + (nt(pick, high) + nt(pick, low))
     for h in range(8):
-        rows = [lse_ref[2 * h : 2 * h + 2, :] * log2e]
-        for n in range(2):
-            cols = pl.ds((2 * h + n) * HD, HD)
-            prod = g_v[:, cols].astype(F32) * o_v[:, cols].astype(F32)
-            rows.append(jnp.sum(prod.T, axis=0, keepdims=True))
-        aux_v[h] = jnp.concatenate(rows + [jnp.zeros((4, ROWS), F32)], axis=0)
+        aux_v[h, 0:2, :] = lse_ref[2 * h : 2 * h + 2, :] * log2e
+        aux_v[h, 2:4, :] = delta[2 * h : 2 * h + 2, :]
+        aux_v[h, 4:8, :] = jnp.zeros((4, ROWS), F32)
     a_copies = []
     for j, (dx, dz) in enumerate(CHUNKS):
         tx, tz = (x + dx) % NX, (z + dz) % 2
@@ -162,8 +167,26 @@
             else:
                 a_copies.append(send(src, dst, a_send.at[at], a_recv.at[at], device(tx, tz, y, (c + dc) % 2)))
 
+    passed = {}
+
+    def chunk_of(j):
+        dx, dz = CHUNKS[j]
+        return 2 * ((x + NX - dx) % NX) + (z + 2 - dz) % 2
+
+    def pass_on(j):
+        for kind, out in enumerate((qh_v, gh_v)):
+            if j == 0:
+                q_copies[j, kind].wait()
+            else:
+                q_copies[j, kind].wait_recv()
+            rows = out.at[chunk_of(j), rows_at(c * ROWS, ROWS), :]
+            at = 2 * j + kind
+            passed[j, kind] = send(rows, rows, s_send.at[at], s_recv.at[at], sibling)
+
     second = {}
-    for dx in ORDER:
+    for n, dx in enumerate(ORDER):
+        for j in PASS[n]:
+            pass_on(j)
         for way, (plane, to) in enumerate((((y + 3) % NY, up), ((y + 1) % NY, down))):
             first[way, dx].wait_recv()
             at = way * NX + dx
@@ -175,22 +198,12 @@
             copy.wait()
         else:
             copy.wait_recv()
-    outs, passed = [], {}
+    outs = []
     for j in range(len(CHUNKS) + 1):
-        if j < len(CHUNKS):
-            dx, dz = CHUNKS[j]
-            i = 2 * ((x + NX - dx) % NX) + (z + 2 - dz) % 2
-            for kind, out in enumerate((qh_v, gh_v)):
-                if j == 0:
-                    q_copies[j, kind].wait()
-                else:
-                    q_copies[j, kind].wait_recv()
-                rows = out.at[i, rows_at(c * ROWS, ROWS), :]
-                at = 2 * j + kind
-                passed[j, kind] = send(rows, rows, s_send.at[at], s_recv.at[at], sibling)
+        if j < len(CHUNKS) and (j, 0) not in passed:
+            pass_on(j)
         if j > 0:
-            dx, dz = CHUNKS[j - 1]
-            i = 2 * ((x + NX - dx) % NX) + (z + 2 - dz) % 2
+            i = chunk_of(j - 1)
             for kind in range(2):
                 passed[j - 1, kind].wait_recv()
             for h in range(2):
@@ -269,32 +282,22 @@
     return jnp.dot(a, b, preferred_element_type=F32)
 
 
-def tile_kernel(part, *refs):
-    if part == 0:
-        (order_ref, lens_ref, q2_ref, g2_ref, qt_ref, gt_ref, lb_ref, db_ref, kv_ref, dq_ref, *dkv_refs), refs = (
-            refs[:14], refs[14:],
-        )
-    else:
-        (order_ref, lens_ref, q2_ref, g2_ref, qt_ref, gt_ref, lb_ref, db_ref, kv_ref, old_ref, dq_ref, *dkv_refs), refs = (
-            refs[:12], refs[12:],
-        )
-    (
-        q_v, g_v, qt_v, gt_v, lb_v, db_v, kv_v, acc_q, acc_k, acc_v, dq_v, dkv_v,
-        s_a, s_b, dp_a, dp_b, p_a, p_b, ds_a, ds_b, tile_q, tile_k, tile_at, tile_cut, sems,
-    ) = refs
+def tile_kernel(
+    order_ref, lens_ref, q2_ref, g2_ref, qt_ref, gt_ref, lb_ref, db_ref, kv_ref,
+    dq_ref, dkv_ref,
+    q_v, g_v, qt_v, gt_v, lb_v, db_v, kv_v, acc_q, acc_k, acc_v, dq_v, dkv_v,
+    s_a, s_b, dp_a, dp_b, p_a, p_b, ds_a, ds_b, tile_q, tile_k, tile_at, tile_cut, sems,
+):
     x, z, y, c = place()
-    core = (c + part) % 2
     loads = [
         pltpu.make_async_copy(src, dst, sems.at[n])
         for n, (src, dst) in enumerate(
             (
-                (kv_ref.at[:, core], kv_v), (q2_ref, q_v), (g2_ref, g_v),
+                (kv_ref, kv_v), (q2_ref, q_v), (g2_ref, g_v),
                 (lb_ref, lb_v), (db_ref, db_v), (qt_ref, qt_v), (gt_ref, gt_v),
             )
         )
     ]
-    if part == 1:
-        loads.append(pltpu.make_async_copy(old_ref, acc_q, sems.at[7]))
     for load in loads:
         load.start()
     starts = [lens_ref[0], lens_ref[0] + lens_ref[1], lens_ref[0] + lens_ref[1] + lens_ref[2]]
@@ -310,8 +313,7 @@
     last_low = [low_of(base[i] + (QT - 1)) for i in range(8)]
 
     def list_slot(slot, count):
-        stored = 4 * (slot // 2) + 2 * core + slot % 2
-        key = order_ref[stored] * BLK + ((x + c + core) % 2) * KT
+        key = order_ref[slot] * BLK + ((x + c + slot // 2) % 2) * KT
         for i in range(8):
             needed = jnp.logical_and(key < base[i] + QT, key + KT > first_low[i])
             whole = jnp.logical_and(key + KT <= base[i] + 1, key >= last_low[i])
@@ -322,7 +324,7 @@
             count = count + needed.astype(jnp.int32)
         return count
 
-    count = lax.fori_loop(0, 8, list_slot, 0)
+    count = lax.fori_loop(0, 16, list_slot, 0)
     for n in range(2):
         tile_q[count + n] = 0
         tile_k[count + n] = 0
@@ -331,22 +333,20 @@
     pairs = (count + 1) // 2
     last = jnp.maximum(2 * pairs - 1, 1)
 
-    for slot in range(8):
-        acc_k[slot] = jnp.zeros((HD, KT), F32)
-        acc_v[slot] = jnp.zeros((HD, KT), F32)
-    if part == 0:
-
-        def clear(i, _):
-            acc_q[i] = jnp.zeros((2 * QT, HD), F32)
-            return 0
-
-        lax.fori_loop(0, 8, clear, 0)
+    def clear(i, _):
+        acc_q[i] = jnp.zeros((2 * QT, HD), F32)
+        for n in range(2):
+            acc_k[2 * i + n] = jnp.zeros((HD, KT), F32)
+            acc_v[2 * i + n] = jnp.zeros((HD, KT), F32)
+        return 0
+
+    lax.fori_loop(0, 8, clear, 0)
 
     def keys(t):
-        return kv_v[tile_k[t] // 2, tile_k[t] % 2, :, 0:HD]
+        return kv_v[tile_k[t], :, 0:HD]
 
     def values(t):
-        return kv_v[tile_k[t] // 2, tile_k[t] % 2, :, HD : 2 * HD]
+        return kv_v[tile_k[t], :, HD : 2 * HD]
 
     def scores(t, s_ref, dp_ref):
         i = tile_q[t]
@@ -441,50 +441,39 @@
 
     lax.fori_loop(0, pairs, pair, 0)
 
-    outs = []
-    if part == 0:
-        outs.append(pltpu.make_async_copy(acc_q, dq_ref, sems.at[0]))
-        outs[0].start()
+    outs = [pltpu.make_async_copy(dq_v, dq_ref, sems.at[0])]
     for d in range(NY):
         plane = (y + d) % NY
+        for q in range(4):
+            slot = 4 * plane + 2 * ((c + q // 2) % 2) + q % 2
+            dkv_v[d, q, 0] = acc_k[slot].astype(BF16)
+            dkv_v[d, q, 1] = acc_v[slot].astype(BF16)
+        outs.append(pltpu.make_async_copy(dkv_v.at[d], dkv_ref.at[d], sems.at[1 + d]))
+        outs[-1].start()
+    for i in range(8):
         for h in range(2):
-            dkv_v[d, h, 0] = acc_k[2 * plane + h].astype(BF16)
-            dkv_v[d, h, 1] = acc_v[2 * plane + h].astype(BF16)
-        out = dkv_refs[d] if part == 0 else dkv_refs[0].at[d]
-        outs.append(pltpu.make_async_copy(dkv_v.at[d], out, sems.at[1 + d]))
-        outs[-1].start()
-    if part == 1:
-
-        def narrow(i, _):
-            for h in range(2):
-                dq_v[h, i] = acc_q[i, h * QT : (h + 1) * QT, :].astype(BF16)
-            return 0
-
-        lax.fori_loop(0, 8, narrow, 0)
-        outs.append(pltpu.make_async_copy(dq_v, dq_ref, sems.at[0]))
-        outs[-1].start()
+            dq_v[h, i] = acc_q[i, h * QT : (h + 1) * QT, :].astype(BF16)
+    outs[0].start()
     for out in outs:
         out.wait()
 
 
-def tiles(part, order, lens, arrays, old=()):
+def tiles(order, lens, *arrays):
     smem = pl.BlockSpec(memory_space=pltpu.SMEM)
     hbm = pl.BlockSpec(memory_space=pl.ANY)
     split = (8, 2 * QT, HD)
     turned = (8, HD, 2 * QT)
     wide = pltpu.VMEM((2 * QT, KT), F32)
     narrow = pltpu.VMEM((2 * QT, KT), BF16)
-    listed = pltpu.SMEM((72,), jnp.int32)
-    sums = (2, 2, HD, KT)
-    if part == 0:
-        out_shape = (jax.ShapeDtypeStruct(split, F32),) + (jax.ShapeDtypeStruct(sums, BF16),) * NY
-    else:
-        out_shape = (jax.ShapeDtypeStruct((2, 8, QT, HD), BF16), jax.ShapeDtypeStruct((NY,) + sums, BF16))
+    listed = pltpu.SMEM((136,), jnp.int32)
     return pl.pallas_call(
-        partial(tile_kernel, part),
-        out_shape=out_shape,
-        in_specs=[smem, smem] + [hbm] * (len(arrays) + len(old)),
-        out_specs=(hbm,) * len(out_shape),
+        tile_kernel,
+        out_shape=(
+            jax.ShapeDtypeStruct((2, 8, QT, HD), BF16),
+            jax.ShapeDtypeStruct((NY, 4, 2, HD, KT), BF16),
+        ),
+        in_specs=[smem, smem] + [hbm] * len(arrays),
+        out_specs=(hbm, hbm),
         scratch_shapes=[
             pltpu.VMEM(split, BF16),
             pltpu.VMEM(split, BF16),
@@ -492,37 +481,36 @@
             pltpu.VMEM(turned, BF16),
             pltpu.VMEM(split, F32),
             pltpu.VMEM(split, F32),
-            pltpu.VMEM((NY, 2, KT, 2 * HD), BF16),
+            pltpu.VMEM((16, KT, 2 * HD), BF16),
             pltpu.VMEM(split, F32),
-            pltpu.VMEM((8, HD, KT), F32),
-            pltpu.VMEM((8, HD, KT), F32),
+            pltpu.VMEM((16, HD, KT), F32),
+            pltpu.VMEM((16, HD, KT), F32),
             pltpu.VMEM((2, 8, QT, HD), BF16),
-            pltpu.VMEM((NY,) + sums, BF16),
+            pltpu.VMEM((NY, 4, 2, HD, KT), BF16),
             wide, wide, wide, wide,
             narrow, narrow, narrow, narrow,
             listed, listed, listed, listed,
-            pltpu.SemaphoreType.DMA((8,)),
+            pltpu.SemaphoreType.DMA((7,)),
         ],
         compiler_params=pltpu.CompilerParams(vmem_limit_bytes=VMEM_LIMIT),
-        cost_estimate=pl.CostEstimate(flops=6 * 10**9, bytes_accessed=16 << 20, transcendentals=4 << 20),
-        name="tiles_a" if part == 0 else "tiles_b",
-    )(order, lens, *arrays, *old)
+        name="tiles",
+    )(order, lens, *arrays)
+
+
+SLOTS = (2, 3, 0, 1)
 
 
 def scatter_kernel(
-    dq_ref, dkv_ref, a0_ref, a1_ref, a2_ref, a3_ref,
+    dq_ref, dkv_ref,
     dq_out, dk_out, dv_out,
-    own, near, land2, send1, land1, fin, mine, theirs, dq_v,
-    load_sem, near_sem, mine_sem, sib_send, sib_recv, s2_send, s2_recv, s1_send, s1_recv, f_send, f_recv, q_send, q_recv,
+    own, land2, send1, land1, fin, mine, theirs, dq_v,
+    load_sem, mine_sem, sib_send, sib_recv, s2_send, s2_recv, s1_send, s1_recv, f_send, f_recv, q_send, q_recv,
 ):
     x, z, y, c = place()
     head = 2 * x + z
     loads = [pltpu.make_async_copy(dkv_ref.at[d], own.at[d], load_sem.at[d]) for d in range(NY)]
-    near_loads = [
-        pltpu.make_async_copy(ref, near.at[n], near_sem.at[n]) for n, ref in enumerate((a0_ref, a1_ref, a2_ref, a3_ref))
-    ]
     mine_load = pltpu.make_async_copy(dq_ref.at[c], mine, mine_sem)
-    for load in [mine_load] + loads + near_loads:
+    for load in [mine_load] + loads:
         load.start()
     enter(x, z, y, c)
     sibling = device(x, z, y, 1 - c)
@@ -536,15 +524,15 @@
         return copy
 
     copies2, copies1 = {}, {}
-    for h in range(2):
+    for h in SLOTS:
         for part, to in enumerate(ways):
-            at = part * 2 + h
+            at = part * 4 + h
             copies2[part, h] = send(dkv_ref.at[2, h, part], land2.at[part, h], s2_send.at[at], s2_recv.at[at], to)
     sib_copy = send(dq_ref.at[1 - c], theirs, sib_send, sib_recv, sibling)
-    for h in range(2):
+    for h in SLOTS:
         for way, to in enumerate(ways):
             part = 1 - way
-            at = (way * 2 + part) * 2 + h
+            at = (way * 2 + part) * 4 + h
             copies1[way, part, h] = send(
                 dkv_ref.at[1 + 2 * way, h, part], land1.at[way, part, h], s1_send.at[at], s1_recv.at[at], to
             )
@@ -570,13 +558,13 @@
 
     for load in loads:
         load.wait()
-    for h in range(2):
+    for h in SLOTS:
         for way, to in enumerate(ways):
             part = way
             copies2[part, h].wait_recv()
             total = own[1 + 2 * way, h, part].astype(F32) + land2[part, h].astype(F32)
             send1[way, h] = total.astype(BF16)
-            at = (way * 2 + part) * 2 + h
+            at = (way * 2 + part) * 4 + h
             copies1[way, part, h] = send(
                 send1.at[way, h], land1.at[way, part, h], s1_send.at[at], s1_recv.at[at], to
             )
@@ -598,23 +586,16 @@
                 to = device((x + dx) % NX, tz, y, (c + dx) % 2)
                 f_copies.append((False, send(src, dst, f_send.at[at], f_recv.at[at], to)))
 
-    for load in near_loads:
-        load.wait()
-    for dx in (2, 0):
+    for dx in (3, 1, 2, 0):
         h = ((x + dx) % NX) // 2
+        q = 2 * (dx % 2) + h
+        if dx in (3, 2):
+            for n in (0, 1):
+                for way in range(2):
+                    for part in range(2):
+                        copies1[way, part, 2 * (dx % 2) + n].wait_recv()
         for part, out in ((0, dk_out), (1, dv_out)):
-            total = near[0, h, part].astype(F32)
-            for n in range(1, 4):
-                total = total + near[n, h, part].astype(F32)
-            final(dx, part, out, total)
-    for h in range(2):
-        for way in range(2):
-            for part in range(2):
-                copies1[way, part, h].wait_recv()
-    for dx in (1, 3):
-        h = ((x + dx) % NX) // 2
-        for part, out in ((0, dk_out), (1, dv_out)):
-            total = own[0, h, part].astype(F32) + land1[0, part, h].astype(F32) + land1[1, part, h].astype(F32)
+            total = own[0, q, part].astype(F32) + land1[0, part, q].astype(F32) + land1[1, part, q].astype(F32)
             final(dx, part, out, total)
 
     for local, copy in q_copies + f_copies:
@@ -639,19 +620,18 @@
         in_specs=[hbm] * len(arrays),
         out_specs=(hbm,) * 3,
         scratch_shapes=[
-            pltpu.VMEM((NY, 2, 2, HD, KT), BF16),
-            pltpu.VMEM((NY, 2, 2, HD, KT), BF16),
-            pltpu.VMEM((2, 2, HD, KT), BF16),
-            pltpu.VMEM((2, 2, HD, KT), BF16),
-            pltpu.VMEM((2, 2, 2, HD, KT), BF16),
+            pltpu.VMEM((NY, 4, 2, HD, KT), BF16),
+            pltpu.VMEM((2, 4, HD, KT), BF16),
+            pltpu.VMEM((2, 4, HD, KT), BF16),
+            pltpu.VMEM((2, 2, 4, HD, KT), BF16),
             pltpu.VMEM((NX, 2, KT, HD), BF16),
             pltpu.VMEM((8, QT, HD), BF16),
             pltpu.VMEM((8, QT, HD), BF16),
             pltpu.VMEM((8, QT, HD), BF16),
-            dma((NY,)), dma((NY,)), dma,
+            dma((NY,)), dma,
             dma, dma,
-            dma((4,)), dma((4,)),
             dma((8,)), dma((8,)),
+            dma((16,)), dma((16,)),
             dma((16,)), dma((16,)),
             dma((16,)), dma((16,)),
         ],
@@ -661,23 +641,28 @@
 
 
 def store_kernel(*refs):
-    count = len(refs) // 2
-    sems = refs[-1]
-    copies = [pltpu.make_async_copy(refs[n], refs[count + n], sems.at[n]) for n in range(count)]
-    for copy in copies:
-        copy.start()
-    for copy in copies:
+    count = len(refs) // 3
+    ins, outs, held, (load_sem, store_sem) = refs[:count], refs[count : 2 * count], refs[2 * count : 3 * count], refs[-2:]
+    loads = [pltpu.make_async_copy(ins[n], held[n], load_sem.at[n]) for n in range(count)]
+    stores = [pltpu.make_async_copy(held[n], outs[n], store_sem.at[n]) for n in range(count)]
+    for load in loads:
+        load.start()
+    for n in range(count):
+        loads[n].wait()
+        stores[n].start()
+    for copy in stores:
         copy.wait()
 
 
 def store(*arrays):
     hbm = pl.BlockSpec(memory_space=pl.ANY)
+    sems = pltpu.SemaphoreType.DMA((len(arrays),))
     return pl.pallas_call(
         store_kernel,
         out_shape=tuple(jax.ShapeDtypeStruct(array.shape, array.dtype) for array in arrays),
         in_specs=[hbm] * len(arrays),
         out_specs=(hbm,) * len(arrays),
-        scratch_shapes=[pltpu.SemaphoreType.DMA((len(arrays),))],
+        scratch_shapes=[pltpu.VMEM(array.shape, array.dtype) for array in arrays] + [sems, sems],
         compiler_params=pltpu.CompilerParams(vmem_limit_bytes=VMEM_LIMIT),
         name="store_grads",
     )(*arrays)
@@ -694,12 +679,8 @@
     doc_lengths,
 ):
     arrays = gather(query_states, key_states, value_states, attn_output, output_grad, logsumexp)
-    dq, *near = tiles(0, block_order, doc_lengths, arrays)
-    for d in (2, 1, 3):
-        pairs = [(2 * plane + core, 2 * ((plane + d) % NY) + core) for plane in range(NY) for core in range(2)]
-        near[d] = lax.ppermute(near[d], "ka", pairs)
-    dq, dkv = tiles(1, block_order, doc_lengths, arrays, (dq,))
-    return store(*scatter(dq, dkv, *near))
+    dq, dkv = tiles(block_order, doc_lengths, *arrays[:-1], arrays[-1].reshape(16, KT, 2 * HD))
+    return store(*scatter(dq, dkv))
 
 
 def solution(mesh):

time: 129 us -> 88.2 us (0.68)
  Pallas kernels: 122 us -> 87.4 us
  starting transfers between devices: 5.42 us -> 0 us
    pallas_call x1, Pallas kernels: 32.9 us -> 2.05 us  [store(): pl.pallas_call(store_kernel, out_shape=tuple((jax.ShapeDtypeStruct(array....]
    pallas_call x2 -> x1, Pallas kernels: 29.2 us -> 21.6 us  [tiles(): pl.pallas_call(tile_kernel, out_shape=(jax.ShapeDtypeStruct((2, 8, QT, HD...]
    pallas_call x1, Pallas kernels: 22.2 us -> 29.6 us  [scatter(): pl.pallas_call(scatter_kernel, out_shape=(jax.ShapeDtypeStruct((ROWS, 204...]
    ppermute x3 -> x0, starting transfers between devices: 5.42 us -> none  [body(): near[d] = lax.ppermute(near[d], 'ka', pairs)]
    pallas_call x1, Pallas kernels: 37.3 us -> 34.1 us  [gather(): pl.pallas_call(gather_kernel, out_shape=tuple((jax.ShapeDtypeStruct(shape...]
  transfers between devices with their start and end apart: 3 -> 0, of which waited for: 0 -> 0; matrix products, arithmetic and copies ran while one was open for 0% -> 0% of each run, Pallas kernels for 11% -> 0%
where the time goes in v4:
time: 88.2 us; the launch traced here: 88 us
  Pallas kernels  87.4 us (99%)
    pallas_call x1, Pallas kernels, gather(): pl.pallas_call(gather_kernel, out_shape=tuple((jax.ShapeDtypeStruct(shape...  34.1 us
    pallas_call x1, Pallas kernels, scatter(): pl.pallas_call(scatter_kernel, out_shape=(jax.ShapeDtypeStruct((ROWS, 204...  29.6 us
    pallas_call x1, Pallas kernels, tiles(): pl.pallas_call(tile_kernel, out_shape=(jax.ShapeDtypeStruct((2, 8, QT, HD...  21.6 us
    pallas_call x1, Pallas kernels, store(): pl.pallas_call(store_kernel, out_shape=tuple((jax.ShapeDtypeStruct(array....  2.05 us

profile of v4, /device:TPU:1, one launch (start us, length us, event | category | flops | bytes accessed | tf_op | source)
XLA Modules:
  0.0 88.0 jit_solution(11838393763658836870)
XLA Ops:
  0.6 34.1 %gather_heads.1 = (bf16[8,512,128]{2,1,0:T(8,128)(2,1)}, bf16[8,512,128]{2,1,0:T(8,128)(2,1)}, bf16[8,128,512]{2,1,0:T(8,128)(2,1)}, bf16[8,128,512]{2,1,0:T(8,1...) custom-call(bf16[128,2048]{1,0:T(8,128)(2,1)} %q_ref.1, ...), custom_call_target="tpu_custom_call" | custom-call | tf_op jit(solution)/shard_map/gather_heads/pallas_call | solution.py:239
  34.8 21.6 %tiles.1 = (bf16[2,8,256,128]{3,2,1,0:T(8,128)(2,1)}, bf16[4,4,2,128,256]{4,3,2,1,0:T(8,128)(2,1)}) custom-call(s32[16]{0:T(128)} %order_ref.1, s32[4]{0:T(128)} %lens_ref.1, bf16[8,512,128]{2,1,0:T(8,128)(2,1)} %get-tuple-element.15.q2_ref, bf16[8,512,128]{2,1,0:T(8,128)(2,1)} %get-tuple-element.16.g2_ref, bf16[8,128,512]{2,1,0:T(8,128)(2,1)} %get-tuple-element.17.qt_ref, ...), custom_call_target="tpu_custom_call" | custom-call | tf_op jit(solution)/shard_map/tiles/pallas_call | solution.py:469
  56.4 29.6 %scatter_grads.1 = (bf16[128,2048]{1,0:T(8,128)(2,1)}, bf16[128,1024]{1,0:T(8,128)(2,1)}, bf16[128,1024]{1,0:T(8,128)(2,1)}) custom-call(bf16[2,8,256,128]{3,2,1,0:T(8,128)(2,1)} %get-tuple-element.22.dq_ref, bf16[4,4,2,128,256]{4,3,2,1,0:T(8,128)(2,1)} %get-tuple-element.23.dkv_ref), custom_call_target="tpu_custom_call" | custom-call | tf_op jit(solution)/shard_map/scatter_grads/pallas_call | solution.py:613
  86.0 2.1 %store_grads.1 = (bf16[128,2048]{1,0:T(8,128)(2,1)}, bf16[128,1024]{1,0:T(8,128)(2,1)}, bf16[128,1024]{1,0:T(8,128)(2,1)}) custom-call(bf16[128,2048]{1,0:T(8,128)(2,1)} %get-tuple-element.24.refs_0_, bf16[128,1024]{1,0:T(8,128)(2,1)} %get-tuple-element.25.refs_1_, bf16[128,1024]{1,0:T(8,128)(2,1)} %get-tuple-element.26.refs_2_), custom_call_target="tpu_custom_call" | custom-call | tf_op jit(solution)/shard_map/store_grads/pallas_call | solution.py:660

commit v5 on v4

--- a/solution.py
+++ b/solution.py
@@ -26,6 +26,7 @@
 QT = 256
 KT = 256
 STEP = 32
+MR = 256
 
 
 def place():
@@ -72,8 +73,8 @@
 
 def gather_kernel(
     q_ref, k_ref, v_ref, o_ref, g_ref, lse_ref,
-    q2_ref, g2_ref, qt_ref, gt_ref, lb_ref, db_ref, kv_ref,
-    o_v, g_v, aux_v, qh_v, gh_v, auxh_v, q2_v, g2_v, qt_v, gt_v, lb_v, db_v,
+    q2_ref, g2_ref, qt_ref, gt_ref, auxh_ref, kv_ref,
+    o_v, g_v, aux_v, qh_v, gh_v, q2_v, g2_v, qt_v, gt_v,
     load_sem, kv_send, kv_recv, y_send, y_recv, y2_send, y2_recv, q_send, q_recv, s_send, s_recv,
     a_send, a_recv, out_sem,
 ):
@@ -161,7 +162,7 @@
     for j, (dx, dz) in enumerate(CHUNKS):
         tx, tz = (x + dx) % NX, (z + dz) % 2
         for dc in range(2):
-            src, dst, at = aux_v.at[2 * tx + tz], auxh_v.at[2 * (2 * x + z) + c], 2 * j + dc
+            src, dst, at = aux_v.at[2 * tx + tz], auxh_ref.at[2 * (2 * x + z) + c], 2 * j + dc
             if at == 0:
                 a_copies.append(keep(src, dst, a_recv.at[at]))
             else:
@@ -212,14 +213,8 @@
                     part = whole[i, :, h * HD : (h + 1) * HD]
                     split[i, rows, :] = part
                     turned[i, :, rows] = part.T
-            for n in range(2):
-                spread = auxh_v[2 * i + n].T
-                for h in range(2):
-                    rows = slice(h * QT + n * ROWS, h * QT + (n + 1) * ROWS)
-                    lb_v[i, rows, :] = jnp.broadcast_to(spread[:, h : h + 1], (ROWS, HD))
-                    db_v[i, rows, :] = jnp.broadcast_to(spread[:, 2 + h : 3 + h], (ROWS, HD))
             for n, (src, dst) in enumerate(
-                ((q2_v, q2_ref), (g2_v, g2_ref), (qt_v, qt_ref), (gt_v, gt_ref), (lb_v, lb_ref), (db_v, db_ref))
+                ((q2_v, q2_ref), (g2_v, g2_ref), (qt_v, qt_ref), (gt_v, gt_ref))
             ):
                 outs.append(keep(src.at[i], dst.at[i], out_sem.at[j - 1, n]))
 
@@ -241,25 +236,22 @@
         out_shape=tuple(
             jax.ShapeDtypeStruct(shape, kind)
             for shape, kind in (
-                (split, BF16), (split, BF16), (turned, BF16), (turned, BF16), (split, F32), (split, F32),
+                (split, BF16), (split, BF16), (turned, BF16), (turned, BF16), ((16, 8, ROWS), F32),
                 ((NY, 2, 2, KT, 2 * HD), BF16),
             )
         ),
         in_specs=[hbm] * 5 + [pl.BlockSpec(memory_space=pltpu.VMEM)],
-        out_specs=(hbm,) * 7,
+        out_specs=(hbm,) * 6,
         scratch_shapes=[
             pltpu.VMEM((ROWS, 2048), BF16),
             pltpu.VMEM((ROWS, 2048), BF16),
             pltpu.VMEM((8, 8, ROWS), F32),
             pltpu.VMEM((8, QT, 2 * HD), BF16),
             pltpu.VMEM((8, QT, 2 * HD), BF16),
-            pltpu.VMEM((16, 8, ROWS), F32),
             pltpu.VMEM(split, BF16),
             pltpu.VMEM(split, BF16),
             pltpu.VMEM(turned, BF16),
             pltpu.VMEM(turned, BF16),
-            pltpu.VMEM(split, F32),
-            pltpu.VMEM(split, F32),
             dma((2,)),
             dma((16,)), dma((16,)),
             dma((8,)), dma((8,)),
@@ -267,7 +259,7 @@
             dma((16,)), dma((16,)),
             dma((16,)), dma((16,)),
             dma((16,)), dma((16,)),
-            dma((8, 6)),
+            dma((8, 4)),
         ],
         compiler_params=pltpu.CompilerParams(collective_id=0, has_side_effects=True, vmem_limit_bytes=VMEM_LIMIT),
         name="gather_heads",
@@ -283,18 +275,17 @@
 
 
 def tile_kernel(
-    order_ref, lens_ref, q2_ref, g2_ref, qt_ref, gt_ref, lb_ref, db_ref, kv_ref,
+    order_ref, lens_ref, q2_ref, g2_ref, qt_ref, gt_ref, aux_ref, kv_ref,
     dq_ref, dkv_ref,
-    q_v, g_v, qt_v, gt_v, lb_v, db_v, kv_v, acc_q, acc_k, acc_v, dq_v, dkv_v,
-    s_a, s_b, dp_a, dp_b, p_a, p_b, ds_a, ds_b, tile_q, tile_k, tile_at, tile_cut, sems,
+    q_v, g_v, qt_v, gt_v, aux_v, lb_v, db_v, kv_v, acc_q, acc_k, acc_v, dq_v, dkv_v,
+    p_a, p_b, ds_a, ds_b, tile_list, cut_list, sems,
 ):
     x, z, y, c = place()
     loads = [
         pltpu.make_async_copy(src, dst, sems.at[n])
         for n, (src, dst) in enumerate(
             (
-                (kv_ref, kv_v), (q2_ref, q_v), (g2_ref, g_v),
-                (lb_ref, lb_v), (db_ref, db_v), (qt_ref, qt_v), (gt_ref, gt_v),
+                (aux_ref, aux_v), (kv_ref, kv_v), (q2_ref, q_v), (g2_ref, g_v), (qt_ref, qt_v), (gt_ref, gt_v),
             )
         )
     ]
@@ -312,24 +303,29 @@
     first_low = [low_of(base[i]) for i in range(8)]
     last_low = [low_of(base[i] + (QT - 1)) for i in range(8)]
 
-    def list_slot(slot, count):
+    def list_slot(slot, counts):
         key = order_ref[slot] * BLK + ((x + c + slot // 2) % 2) * KT
+        wholes, cuts = counts
         for i in range(8):
             needed = jnp.logical_and(key < base[i] + QT, key + KT > first_low[i])
             whole = jnp.logical_and(key + KT <= base[i] + 1, key >= last_low[i])
-            tile_q[count] = i
-            tile_k[count] = slot
-            tile_at[count] = key - base[i]
-            tile_cut[count] = jnp.where(whole, 0, 1)
-            count = count + needed.astype(jnp.int32)
-        return count
-
-    count = lax.fori_loop(0, 16, list_slot, 0)
+            entry = slot * 8 + i
+            tile_list[wholes] = entry
+            cut_list[cuts] = entry
+            wholes = wholes + jnp.logical_and(needed, whole).astype(jnp.int32)
+            cuts = cuts + jnp.logical_and(needed, jnp.logical_not(whole)).astype(jnp.int32)
+        return wholes, cuts
+
+    wholes, cuts = lax.fori_loop(0, 16, list_slot, (0, 0))
+
+    def append(n, _):
+        tile_list[wholes + n] = cut_list[n]
+        return 0
+
+    lax.fori_loop(0, cuts, append, 0)
+    count = wholes + cuts
     for n in range(2):
-        tile_q[count + n] = 0
-        tile_k[count + n] = 0
-        tile_at[count + n] = 1 << 20
-        tile_cut[count + n] = 1
+        tile_list[count + n] = 0
     pairs = (count + 1) // 2
     last = jnp.maximum(2 * pairs - 1, 1)
 
@@ -343,36 +339,32 @@
     lax.fori_loop(0, 8, clear, 0)
 
     def keys(t):
-        return kv_v[tile_k[t], :, 0:HD]
+        return kv_v[tile_list[t] // 8, :, 0:HD]
 
     def values(t):
-        return kv_v[tile_k[t], :, HD : 2 * HD]
-
-    def scores(t, s_ref, dp_ref):
-        i = tile_q[t]
-
-        def piece(out, left, right, h):
-            rows = slice(h * QT, (h + 1) * QT)
-            out[rows, :] = nt(left[i, rows, :], right(t))
-
-        return [
-            partial(piece, out, left, right, h)
-            for out, left, right in ((s_ref, q_v, keys), (dp_ref, g_v, values))
-            for h in range(2)
-        ]
-
-    def weigh(t, s_ref, dp_ref, p_ref, ds_ref, cut):
-        i, at = tile_q[t], tile_at[t]
+        return kv_v[tile_list[t] // 8, :, HD : 2 * HD]
+
+    def weigh(t, p_ref, ds_ref, cut):
+        i, slot = tile_list[t] % 8, tile_list[t] // 8
         if cut:
             query_base = order_ref[2 * i + y // 2] * BLK + (y % 2) * QT
+            at = order_ref[slot] * BLK + ((x + c + slot // 2) % 2) * KT - query_base
+            at = jnp.where(t < count, at, 1 << 20)
         step = STEP
+        held = {}
+
+        def score(n):
+            rows = slice(n * MR, (n + 1) * MR)
+            held[n] = (nt(q_v[i, rows, :], keys(t)), nt(g_v[i, rows, :], values(t)))
 
         def piece(r):
+            n, o = r // MR, r % MR
+            raw, dprob = held[n][0][o : o + step], held[n][1][o : o + step]
             lse = lb_v[i, r : r + step, :]
             delta = db_v[i, r : r + step, :]
             lse = jnp.concatenate([lse] * (KT // HD), axis=1)
             delta = jnp.concatenate([delta] * (KT // HD), axis=1)
-            th = jnp.tanh(s_ref[r : r + step, :] * (score_scale / softcap))
+            th = jnp.tanh(raw * (score_scale / softcap))
             p = jnp.exp2(th * (softcap * log2e) - lse)
             if cut:
                 row = lax.broadcasted_iota(jnp.int32, (step, HD), 0) + r % QT
@@ -381,14 +373,20 @@
                 low = jnp.concatenate([low] * (KT // HD), axis=1)
                 key = lax.broadcasted_iota(jnp.int32, (step, KT), 1) + at
                 p = jnp.where((key <= row) & (key >= low), p, 0.0)
-            ds = p * (dp_ref[r : r + step, :] - delta) * ((1.0 - th * th) * score_scale)
+            ds = p * (dprob - delta) * ((1.0 - th * th) * score_scale)
             p_ref[r : r + step, :] = p.astype(BF16)
             ds_ref[r : r + step, :] = ds.astype(BF16)
 
-        return [partial(piece, r) for r in range(0, 2 * QT, step)]
+        count_m = 2 * QT // MR
+        out = [partial(score, 0)]
+        for n in range(count_m):
+            if n + 1 < count_m:
+                out.append(partial(score, n + 1))
+            out += [partial(piece, r) for r in range(n * MR, (n + 1) * MR, step)]
+        return out
 
     def gradients(t, p_ref, ds_ref):
-        i, slot = tile_q[t], tile_k[t]
+        i, slot = tile_list[t] % 8, tile_list[t] // 8
 
         def key_piece(out, left, right):
             out[slot] += nn(left[i], right[...])
@@ -409,35 +407,36 @@
         for _, _, piece in sorted(marked, key=lambda entry: entry[:2]):
             piece()
 
-    buffers = ((s_a, dp_a, p_a, ds_a), (s_b, dp_b, p_b, ds_b))
-
-    def step(t, parity):
-        s0, dp0, p0, ds0 = buffers[parity]
-        s1, dp1, p1, ds1 = buffers[1 - parity]
-        middle = jnp.minimum(t + 1, last)
-
-        def whole_step(cut):
-            run(
-                scores(jnp.minimum(t + 2, last), s0, dp0) + gradients(t, p0, ds0),
-                weigh(middle, s1, dp1, p1, ds1, cut),
-            )
-
-        pl.when(tile_cut[middle] == 0)(lambda: whole_step(False))
-        pl.when(tile_cut[middle] != 0)(lambda: whole_step(True))
-
-    for load in loads[:3]:
+    def step(t, old, new, cut):
+        run(weigh(jnp.minimum(t + 1, last), *new, cut), gradients(t, *old))
+
+    def pair(n, _):
+        def steps(cut):
+            step(2 * n, (p_a, ds_a), (p_b, ds_b), cut)
+            step(2 * n + 1, (p_b, ds_b), (p_a, ds_a), cut)
+
+        whole = 2 * n + 2 < wholes
+        pl.when(whole)(lambda: steps(False))
+        pl.when(jnp.logical_not(whole))(lambda: steps(True))
+        return 0
+
+    loads[0].wait()
+
+    def spread_chunk(i, _):
+        for n in range(2):
+            turned = aux_v[2 * i + n].T
+            for h in range(2):
+                rows = slice(h * QT + n * ROWS, h * QT + (n + 1) * ROWS)
+                lb_v[i, rows, :] = jnp.broadcast_to(turned[:, h : h + 1], (ROWS, HD))
+                db_v[i, rows, :] = jnp.broadcast_to(turned[:, 2 + h : 3 + h], (ROWS, HD))
+        return 0
+
+    lax.fori_loop(0, 8, spread_chunk, 0)
+    for load in loads[1:4]:
         load.wait()
-    run(scores(0, s_a, dp_a))
-    for load in loads[3:5]:
+    run(weigh(0, p_a, ds_a, True))
+    for load in loads[4:]:
         load.wait()
-    run(scores(1, s_b, dp_b), weigh(0, s_a, dp_a, p_a, ds_a, True))
-    for load in loads[5:]:
-        load.wait()
-
-    def pair(n, _):
-        step(2 * n, 0)
-        step(2 * n + 1, 1)
-        return 0
 
     lax.fori_loop(0, pairs, pair, 0)
 
@@ -463,7 +462,6 @@
     hbm = pl.BlockSpec(memory_space=pl.ANY)
     split = (8, 2 * QT, HD)
     turned = (8, HD, 2 * QT)
-    wide = pltpu.VMEM((2 * QT, KT), F32)
     narrow = pltpu.VMEM((2 * QT, KT), BF16)
     listed = pltpu.SMEM((136,), jnp.int32)
     return pl.pallas_call(
@@ -479,6 +477,7 @@
             pltpu.VMEM(split, BF16),
             pltpu.VMEM(turned, BF16),
             pltpu.VMEM(turned, BF16),
+            pltpu.VMEM((16, 8, ROWS), F32),
             pltpu.VMEM(split, F32),
             pltpu.VMEM(split, F32),
             pltpu.VMEM((16, KT, 2 * HD), BF16),
@@ -487,9 +486,8 @@
             pltpu.VMEM((16, HD, KT), F32),
             pltpu.VMEM((2, 8, QT, HD), BF16),
             pltpu.VMEM((NY, 4, 2, HD, KT), BF16),
-            wide, wide, wide, wide,
             narrow, narrow, narrow, narrow,
-            listed, listed, listed, listed,
+            listed, listed,
             pltpu.SemaphoreType.DMA((7,)),
         ],
         compiler_params=pltpu.CompilerParams(vmem_limit_bytes=VMEM_LIMIT),

time: 88.2 us -> 85.7 us (0.972)
  Pallas kernels: 87.4 us -> 84.9 us
    pallas_call x1, Pallas kernels: 34.1 us -> 33 us  [gather(): pl.pallas_call(gather_kernel, out_shape=tuple((jax.ShapeDtypeStruct(shape...]
    pallas_call x1, Pallas kernels: 21.6 us -> 20.5 us  [tiles(): pl.pallas_call(tile_kernel, out_shape=(jax.ShapeDtypeStruct((2, 8, QT, HD...]
where the time goes in v5:
time: 85.7 us; the launch traced here: 85.5 us
  Pallas kernels  84.9 us (99%)
    pallas_call x1, Pallas kernels, gather(): pl.pallas_call(gather_kernel, out_shape=tuple((jax.ShapeDtypeStruct(shape...  33 us
    pallas_call x1, Pallas kernels, scatter(): pl.pallas_call(scatter_kernel, out_shape=(jax.ShapeDtypeStruct((ROWS, 204...  29.4 us
    pallas_call x1, Pallas kernels, tiles(): pl.pallas_call(tile_kernel, out_shape=(jax.ShapeDtypeStruct((2, 8, QT, HD...  20.5 us
    pallas_call x1, Pallas kernels, store(): pl.pallas_call(store_kernel, out_shape=tuple((jax.ShapeDtypeStruct(array....  2.05 us

profile of v5, /device:TPU:1, one launch (start us, length us, event | category | flops | bytes accessed | tf_op | source)
XLA Modules:
  0.0 85.5 jit_solution(1133241187891897375)
XLA Ops:
  0.6 33.0 %gather_heads.1 = (bf16[8,512,128]{2,1,0:T(8,128)(2,1)}, bf16[8,512,128]{2,1,0:T(8,128)(2,1)}, bf16[8,128,512]{2,1,0:T(8,128)(2,1)}, bf16[8,128,512]{2,1,0:T(8,1...) custom-call(bf16[128,2048]{1,0:T(8,128)(2,1)} %q_ref.1, bf16[128,1024]{1,0:T(8,128)(2,1)} %k_ref.1, ...), custom_call_target="tpu_custom_call" | custom-call | tf_op jit(solution)/shard_map/gather_heads/pallas_call | solution.py:234
  33.6 20.5 %tiles.1 = (bf16[2,8,256,128]{3,2,1,0:T(8,128)(2,1)}, bf16[4,4,2,128,256]{4,3,2,1,0:T(8,128)(2,1)}) custom-call(s32[16]{0:T(128)} %order_ref.1, s32[4]{0:T(128)} %lens_ref.1, bf16[8,512,128]{2,1,0:T(8,128)(2,1)} %get-tuple-element.14.q2_ref, bf16[8,512,128]{2,1,0:T(8,128)(2,1)} %get-tuple-element.15.g2_ref, bf16[8,128,512]{2,1,0:T(8,128)(2,1)} %get-tuple-element.16.qt_ref, ...), custom_call_target="tpu_custom_call" | custom-call | tf_op jit(solution)/shard_map/tiles/pallas_call | solution.py:467
  54.1 29.4 %scatter_grads.1 = (bf16[128,2048]{1,0:T(8,128)(2,1)}, bf16[128,1024]{1,0:T(8,128)(2,1)}, bf16[128,1024]{1,0:T(8,128)(2,1)}) custom-call(bf16[2,8,256,128]{3,2,1,0:T(8,128)(2,1)} %get-tuple-element.20.dq_ref, bf16[4,4,2,128,256]{4,3,2,1,0:T(8,128)(2,1)} %get-tuple-element.21.dkv_ref), custom_call_target="tpu_custom_call" | custom-call | tf_op jit(solution)/shard_map/scatter_grads/pallas_call | solution.py:611
  83.5 2.1 %store_grads.1 = (bf16[128,2048]{1,0:T(8,128)(2,1)}, bf16[128,1024]{1,0:T(8,128)(2,1)}, bf16[128,1024]{1,0:T(8,128)(2,1)}) custom-call(bf16[128,2048]{1,0:T(8,128)(2,1)} %get-tuple-element.22.refs_0_, bf16[128,1024]{1,0:T(8,128)(2,1)} %get-tuple-element.23.refs_1_, bf16[128,1024]{1,0:T(8,128)(2,1)} %get-tuple-element.24.refs_2_), custom_call_target="tpu_custom_call" | custom-call | tf_op jit(solution)/shard_map/store_grads/pallas_call | solution.py:658

commit v6 on v5

--- a/solution.py
+++ b/solution.py
@@ -115,6 +115,14 @@
                     to = device(tx, tz, y, (c + dx) % 2)
                     kv_copies[dx, dz, part] = send(src, dst, kv_send.at[at], kv_recv.at[at], to)
 
+    own_rows = kv_ref.at[y, c, x // 2, rows_at(z * ROWS, ROWS), :]
+    other_rows = kv_ref.at[y, c, x // 2, rows_at((1 - z) * ROWS, ROWS), :]
+    kv_copies[0, 0, 0].wait()
+    kv_copies[0, 0, 1].wait()
+    own_first = [
+        send(own_rows, own_rows, y_send.at[8 + way], y_recv.at[8 + way], to) for way, to in enumerate((up, down))
+    ]
+
     def block(plane, dx):
         return plane, (c + dx) % 2, ((x + NX - dx) % NX) // 2
 
@@ -122,12 +130,9 @@
     for dx in ORDER:
         for dz in range(2):
             for part in range(2):
-                copy = kv_copies[dx, dz, part]
-                if dx == 0 and dz == 0:
-                    copy.wait()
-                else:
-                    copy.wait_recv()
-        rows = kv_ref.at[block(y, dx)]
+                if dx != 0 or dz != 0:
+                    kv_copies[dx, dz, part].wait_recv()
+        rows = other_rows if dx == 0 else kv_ref.at[block(y, dx)]
         for way, to in ((0, up), (1, down)):
             at = way * NX + dx
             first[way, dx] = send(rows, rows, y_send.at[at], y_recv.at[at], to)
@@ -190,6 +195,8 @@
             pass_on(j)
         for way, (plane, to) in enumerate((((y + 3) % NY, up), ((y + 1) % NY, down))):
             first[way, dx].wait_recv()
+            if dx == 0:
+                own_first[way].wait_recv()
             at = way * NX + dx
             half = kv_ref.at[block(plane, dx)].at[:, pl.ds(way * HD, HD)]
             second[way, dx] = send(half, half, y2_send.at[at], y2_recv.at[at], to)
@@ -254,7 +261,7 @@
             pltpu.VMEM(turned, BF16),
             dma((2,)),
             dma((16,)), dma((16,)),
-            dma((8,)), dma((8,)),
+            dma((10,)), dma((10,)),
             dma((8,)), dma((8,)),
             dma((16,)), dma((16,)),
             dma((16,)), dma((16,)),
@@ -316,7 +323,19 @@
             cuts = cuts + jnp.logical_and(needed, jnp.logical_not(whole)).astype(jnp.int32)
         return wholes, cuts
 
-    wholes, cuts = lax.fori_loop(0, 16, list_slot, (0, 0))
+    def prepare(slot, counts):
+        turned = aux_v[slot].T
+        for h in range(2):
+            rows = pl.ds(pl.multiple_of(h * QT + (slot % 2) * ROWS, ROWS), ROWS)
+            lb_v[slot // 2, rows, :] = jnp.broadcast_to(turned[:, h : h + 1], (ROWS, HD))
+            db_v[slot // 2, rows, :] = jnp.broadcast_to(turned[:, 2 + h : 3 + h], (ROWS, HD))
+            acc_q[slot // 2, rows, :] = jnp.zeros((ROWS, HD), F32)
+        acc_k[slot] = jnp.zeros((HD, KT), F32)
+        acc_v[slot] = jnp.zeros((HD, KT), F32)
+        return list_slot(slot, counts)
+
+    loads[0].wait()
+    wholes, cuts = lax.fori_loop(0, 16, prepare, (0, 0), unroll=16)
 
     def append(n, _):
         tile_list[wholes + n] = cut_list[n]
@@ -328,15 +347,6 @@
         tile_list[count + n] = 0
     pairs = (count + 1) // 2
     last = jnp.maximum(2 * pairs - 1, 1)
-
-    def clear(i, _):
-        acc_q[i] = jnp.zeros((2 * QT, HD), F32)
-        for n in range(2):
-            acc_k[2 * i + n] = jnp.zeros((HD, KT), F32)
-            acc_v[2 * i + n] = jnp.zeros((HD, KT), F32)
-        return 0
-
-    lax.fori_loop(0, 8, clear, 0)
 
     def keys(t):
         return kv_v[tile_list[t] // 8, :, 0:HD]
@@ -420,18 +430,6 @@
         pl.when(jnp.logical_not(whole))(lambda: steps(True))
         return 0
 
-    loads[0].wait()
-
-    def spread_chunk(i, _):
-        for n in range(2):
-            turned = aux_v[2 * i + n].T
-            for h in range(2):
-                rows = slice(h * QT + n * ROWS, h * QT + (n + 1) * ROWS)
-                lb_v[i, rows, :] = jnp.broadcast_to(turned[:, h : h + 1], (ROWS, HD))
-                db_v[i, rows, :] = jnp.broadcast_to(turned[:, 2 + h : 3 + h], (ROWS, HD))
-        return 0
-
-    lax.fori_loop(0, 8, spread_chunk, 0)
     for load in loads[1:4]:
         load.wait()
     run(weigh(0, p_a, ds_a, True))
@@ -495,7 +493,7 @@
     )(order, lens, *arrays)
 
 
-SLOTS = (2, 3, 0, 1)
+SLOTS = (3, 1, 2, 0)
 
 
 def scatter_kernel(
@@ -522,17 +520,18 @@
         return copy
 
     copies2, copies1 = {}, {}
+    slot = {dx: 2 * (dx % 2) + ((x + dx) % NX) // 2 for dx in SLOTS}
     for h in SLOTS:
         for part, to in enumerate(ways):
             at = part * 4 + h
-            copies2[part, h] = send(dkv_ref.at[2, h, part], land2.at[part, h], s2_send.at[at], s2_recv.at[at], to)
+            copies2[part, h] = send(dkv_ref.at[2, slot[h], part], land2.at[part, h], s2_send.at[at], s2_recv.at[at], to)
     sib_copy = send(dq_ref.at[1 - c], theirs, sib_send, sib_recv, sibling)
     for h in SLOTS:
         for way, to in enumerate(ways):
             part = 1 - way
             at = (way * 2 + part) * 4 + h
             copies1[way, part, h] = send(
-                dkv_ref.at[1 + 2 * way, h, part], land1.at[way, part, h], s1_send.at[at], s1_recv.at[at], to
+                dkv_ref.at[1 + 2 * way, slot[h], part], land1.at[way, part, h], s1_send.at[at], s1_recv.at[at], to
             )
 
     mine_load.wait()
@@ -560,7 +559,7 @@
         for way, to in enumerate(ways):
             part = way
             copies2[part, h].wait_recv()
-            total = own[1 + 2 * way, h, part].astype(F32) + land2[part, h].astype(F32)
+            total = own[1 + 2 * way, slot[h], part].astype(F32) + land2[part, h].astype(F32)
             send1[way, h] = total.astype(BF16)
             at = (way * 2 + part) * 4 + h
             copies1[way, part, h] = send(
@@ -584,16 +583,11 @@
                 to = device((x + dx) % NX, tz, y, (c + dx) % 2)
                 f_copies.append((False, send(src, dst, f_send.at[at], f_recv.at[at], to)))
 
-    for dx in (3, 1, 2, 0):
-        h = ((x + dx) % NX) // 2
-        q = 2 * (dx % 2) + h
-        if dx in (3, 2):
-            for n in (0, 1):
-                for way in range(2):
-                    for part in range(2):
-                        copies1[way, part, 2 * (dx % 2) + n].wait_recv()
+    for dx in SLOTS:
         for part, out in ((0, dk_out), (1, dv_out)):
-            total = own[0, q, part].astype(F32) + land1[0, part, q].astype(F32) + land1[1, part, q].astype(F32)
+            for way in range(2):
+                copies1[way, part, dx].wait_recv()
+            total = own[0, slot[dx], part].astype(F32) + land1[0, part, dx].astype(F32) + land1[1, part, dx].astype(F32)
             final(dx, part, out, total)
 
     for local, copy in q_copies + f_copies:

time: 85.7 us -> 84.6 us (0.987)
  the two profiles are of different devices: /device:TPU:1 before, /device:TPU:65 now
where the time goes in v6:
time: 84.6 us; the launch traced here: 84.4 us
  Pallas kernels  83.7 us (99%)
    pallas_call x1, Pallas kernels, scatter(): pl.pallas_call(scatter_kernel, out_shape=(jax.ShapeDtypeStruct((ROWS, 204...  36.4 us
    pallas_call x1, Pallas kernels, gather(): pl.pallas_call(gather_kernel, out_shape=tuple((jax.ShapeDtypeStruct(shape...  31.1 us
    pallas_call x1, Pallas kernels, tiles(): pl.pallas_call(tile_kernel, out_shape=(jax.ShapeDtypeStruct((2, 8, QT, HD...  14.2 us
    pallas_call x1, Pallas kernels, store(): pl.pallas_call(store_kernel, out_shape=tuple((jax.ShapeDtypeStruct(array....  2.05 us

profile of v6, /device:TPU:65, one launch (start us, length us, event | category | flops | bytes accessed | tf_op | source)
XLA Modules:
  0.0 84.4 jit_solution(14373930263158650602)
XLA Ops:
  0.6 31.1 %gather_heads.1 = (bf16[8,512,128]{2,1,0:T(8,128)(2,1)}, bf16[8,512,128]{2,1,0:T(8,128)(2,1)}, bf16[8,128,512]{2,1,0:T(8,128)(2,1)}, bf16[8,128,512]{2,1,0:T(8,1...) custom-call(bf16[128,2048]{1,0:T(8,128)(2,1)} %q_ref.1, bf16[128,1024]{1,0:T(8,128)(2,1)} %k_ref.1, ...), custom_call_target="tpu_custom_call" | custom-call | tf_op jit(solution)/shard_map/gather_heads/pallas_call | solution.py:241
  31.7 14.2 %tiles.1 = (bf16[2,8,256,128]{3,2,1,0:T(8,128)(2,1)}, bf16[4,4,2,128,256]{4,3,2,1,0:T(8,128)(2,1)}) custom-call(s32[16]{0:T(128)} %order_ref.1, s32[4]{0:T(128)} %lens_ref.1, bf16[8,512,128]{2,1,0:T(8,128)(2,1)} %get-tuple-element.14.q2_ref, bf16[8,512,128]{2,1,0:T(8,128)(2,1)} %get-tuple-element.15.g2_ref, bf16[8,128,512]{2,1,0:T(8,128)(2,1)} %get-tuple-element.16.qt_ref, ...), custom_call_target="tpu_custom_call" | custom-call | tf_op jit(solution)/shard_map/tiles/pallas_call | solution.py:465
  45.9 36.4 %scatter_grads.1 = (bf16[128,2048]{1,0:T(8,128)(2,1)}, bf16[128,1024]{1,0:T(8,128)(2,1)}, bf16[128,1024]{1,0:T(8,128)(2,1)}) custom-call(bf16[2,8,256,128]{3,2,1,0:T(8,128)(2,1)} %get-tuple-element.20.dq_ref, bf16[4,4,2,128,256]{4,3,2,1,0:T(8,128)(2,1)} %get-tuple-element.21.dkv_ref), custom_call_target="tpu_custom_call" | custom-call | tf_op jit(solution)/shard_map/scatter_grads/pallas_call | solution.py:605
  82.3 2.1 %store_grads.1 = (bf16[128,2048]{1,0:T(8,128)(2,1)}, bf16[128,1024]{1,0:T(8,128)(2,1)}, bf16[128,1024]{1,0:T(8,128)(2,1)}) custom-call(bf16[128,2048]{1,0:T(8,128)(2,1)} %get-tuple-element.22.refs_0_, bf16[128,1024]{1,0:T(8,128)(2,1)} %get-tuple-element.23.refs_1_, bf16[128,1024]{1,0:T(8,128)(2,1)} %get-tuple-element.24.refs_2_), custom_call_target="tpu_custom_call" | custom-call | tf_op jit(solution)/shard_map/store_grads/pallas_call | solution.py:652

commit v7 on v6

--- a/solution.py
+++ b/solution.py
@@ -26,7 +26,6 @@
 QT = 256
 KT = 256
 STEP = 32
-MR = 256
 
 
 def place():
@@ -73,10 +72,10 @@
 
 def gather_kernel(
     q_ref, k_ref, v_ref, o_ref, g_ref, lse_ref,
-    q2_ref, g2_ref, qt_ref, gt_ref, auxh_ref, kv_ref,
-    o_v, g_v, aux_v, qh_v, gh_v, q2_v, g2_v, qt_v, gt_v,
+    qh_ref, gh_ref, auxh_ref, kv_ref,
+    o_v, g_v, aux_v,
     load_sem, kv_send, kv_recv, y_send, y_recv, y2_send, y2_recv, q_send, q_recv, s_send, s_recv,
-    a_send, a_recv, out_sem,
+    a_send, a_recv,
 ):
     x, z, y, c = place()
     loads = [
@@ -140,7 +139,7 @@
             if dx != 0:
                 continue
             tx, tz = (x + jx) % NX, (z + jz) % 2
-            for kind, (ref, out) in enumerate(((q_ref, qh_v), (g_ref, gh_v))):
+            for kind, (ref, out) in enumerate(((q_ref, qh_ref), (g_ref, gh_ref))):
                 src = ref.at[:, columns(2 * (2 * tx + tz), 2)]
                 dst = out.at[2 * x + z, rows_at(c * ROWS, ROWS), :]
                 at = 2 * j + kind
@@ -180,7 +179,7 @@
         return 2 * ((x + NX - dx) % NX) + (z + 2 - dz) % 2
 
     def pass_on(j):
-        for kind, out in enumerate((qh_v, gh_v)):
+        for kind, out in enumerate((qh_ref, gh_ref)):
             if j == 0:
                 q_copies[j, kind].wait()
             else:
@@ -201,64 +200,41 @@
             half = kv_ref.at[block(plane, dx)].at[:, pl.ds(way * HD, HD)]
             second[way, dx] = send(half, half, y2_send.at[at], y2_recv.at[at], to)
 
+    for j in range(len(CHUNKS)):
+        if (j, 0) not in passed:
+            pass_on(j)
     for n, copy in enumerate(a_copies):
         if n == 0:
             copy.wait()
         else:
             copy.wait_recv()
-    outs = []
-    for j in range(len(CHUNKS) + 1):
-        if j < len(CHUNKS) and (j, 0) not in passed:
-            pass_on(j)
-        if j > 0:
-            i = chunk_of(j - 1)
-            for kind in range(2):
-                passed[j - 1, kind].wait_recv()
-            for h in range(2):
-                rows = slice(h * QT, (h + 1) * QT)
-                for whole, split, turned in ((qh_v, q2_v, qt_v), (gh_v, g2_v, gt_v)):
-                    part = whole[i, :, h * HD : (h + 1) * HD]
-                    split[i, rows, :] = part
-                    turned[i, :, rows] = part.T
-            for n, (src, dst) in enumerate(
-                ((q2_v, q2_ref), (g2_v, g2_ref), (qt_v, qt_ref), (gt_v, gt_ref))
-            ):
-                outs.append(keep(src.at[i], dst.at[i], out_sem.at[j - 1, n]))
-
+    for copy in passed.values():
+        copy.wait_recv()
     for copy in second.values():
         copy.wait_recv()
     for copy in sends:
         copy.wait_send()
-    for copy in outs:
-        copy.wait()
 
 
 def gather(q, k, v, o, g, lse):
     hbm = pl.BlockSpec(memory_space=pl.ANY)
     dma = pltpu.SemaphoreType.DMA
-    split = (8, 2 * QT, HD)
-    turned = (8, HD, 2 * QT)
+    both = (8, QT, 2 * HD)
     return pl.pallas_call(
         gather_kernel,
         out_shape=tuple(
             jax.ShapeDtypeStruct(shape, kind)
             for shape, kind in (
-                (split, BF16), (split, BF16), (turned, BF16), (turned, BF16), ((16, 8, ROWS), F32),
+                (both, BF16), (both, BF16), ((16, 8, ROWS), F32),
                 ((NY, 2, 2, KT, 2 * HD), BF16),
             )
         ),
         in_specs=[hbm] * 5 + [pl.BlockSpec(memory_space=pltpu.VMEM)],
-        out_specs=(hbm,) * 6,
+        out_specs=(hbm,) * 4,
         scratch_shapes=[
             pltpu.VMEM((ROWS, 2048), BF16),
             pltpu.VMEM((ROWS, 2048), BF16),
             pltpu.VMEM((8, 8, ROWS), F32),
-            pltpu.VMEM((8, QT, 2 * HD), BF16),
-            pltpu.VMEM((8, QT, 2 * HD), BF16),
-            pltpu.VMEM(split, BF16),
-            pltpu.VMEM(split, BF16),
-            pltpu.VMEM(turned, BF16),
-            pltpu.VMEM(turned, BF16),
             dma((2,)),
             dma((16,)), dma((16,)),
             dma((10,)), dma((10,)),
@@ -266,7 +242,6 @@
             dma((16,)), dma((16,)),
             dma((16,)), dma((16,)),
             dma((16,)), dma((16,)),
-            dma((8, 4)),
         ],
         compiler_params=pltpu.CompilerParams(collective_id=0, has_side_effects=True, vmem_limit_bytes=VMEM_LIMIT),
         name="gather_heads",
@@ -282,7 +257,7 @@
 
 
 def tile_kernel(
-    order_ref, lens_ref, q2_ref, g2_ref, qt_ref, gt_ref, aux_ref, kv_ref,
+    order_ref, lens_ref, qh_ref, gh_ref, aux_ref, kv_ref,
     dq_ref, dkv_ref,
     q_v, g_v, qt_v, gt_v, aux_v, lb_v, db_v, kv_v, acc_q, acc_k, acc_v, dq_v, dkv_v,
     p_a, p_b, ds_a, ds_b, tile_list, cut_list, sems,
@@ -292,7 +267,7 @@
         pltpu.make_async_copy(src, dst, sems.at[n])
         for n, (src, dst) in enumerate(
             (
-                (aux_ref, aux_v), (kv_ref, kv_v), (q2_ref, q_v), (g2_ref, g_v), (qt_ref, qt_v), (gt_ref, gt_v),
+                (aux_ref, aux_v), (qh_ref, q_v), (gh_ref, g_v), (kv_ref, kv_v),
             )
         )
     ]
@@ -364,11 +339,11 @@
         held = {}
 
         def score(n):
-            rows = slice(n * MR, (n + 1) * MR)
-            held[n] = (nt(q_v[i, rows, :], keys(t)), nt(g_v[i, rows, :], values(t)))
+            cols = slice(n * HD, (n + 1) * HD)
+            held[n] = (nt(q_v[i, :, cols], keys(t)), nt(g_v[i, :, cols], values(t)))
 
         def piece(r):
-            n, o = r // MR, r % MR
+            n, o = r // QT, r % QT
             raw, dprob = held[n][0][o : o + step], held[n][1][o : o + step]
             lse = lb_v[i, r : r + step, :]
             delta = db_v[i, r : r + step, :]
@@ -387,13 +362,7 @@
             p_ref[r : r + step, :] = p.astype(BF16)
             ds_ref[r : r + step, :] = ds.astype(BF16)
 
-        count_m = 2 * QT // MR
-        out = [partial(score, 0)]
-        for n in range(count_m):
-            if n + 1 < count_m:
-                out.append(partial(score, n + 1))
-            out += [partial(piece, r) for r in range(n * MR, (n + 1) * MR, step)]
-        return out
+        return [partial(score, 0), partial(score, 1)] + [partial(piece, r) for r in range(0, 2 * QT, step)]
 
     def gradients(t, p_ref, ds_ref):
         i, slot = tile_list[t] % 8, tile_list[t] // 8
@@ -430,11 +399,13 @@
         pl.when(jnp.logical_not(whole))(lambda: steps(True))
         return 0
 
-    for load in loads[1:4]:
-        load.wait()
+    for kind, (whole, turned) in enumerate(((q_v, qt_v), (g_v, gt_v))):
+        loads[1 + kind].wait()
+        for i in range(8):
+            for h in range(2):
+                turned[i, :, h * QT : (h + 1) * QT] = whole[i, :, h * HD : (h + 1) * HD].T
+    loads[3].wait()
     run(weigh(0, p_a, ds_a, True))
-    for load in loads[4:]:
-        load.wait()
 
     lax.fori_loop(0, pairs, pair, 0)
 
@@ -471,8 +442,8 @@
         in_specs=[smem, smem] + [hbm] * len(arrays),
         out_specs=(hbm, hbm),
         scratch_shapes=[
-            pltpu.VMEM(split, BF16),
-            pltpu.VMEM(split, BF16),
+            pltpu.VMEM((8, QT, 2 * HD), BF16),
+            pltpu.VMEM((8, QT, 2 * HD), BF16),
             pltpu.VMEM(turned, BF16),
             pltpu.VMEM(turned, BF16),
             pltpu.VMEM((16, 8, ROWS), F32),
@@ -486,7 +457,7 @@
             pltpu.VMEM((NY, 4, 2, HD, KT), BF16),
             narrow, narrow, narrow, narrow,
             listed, listed,
-            pltpu.SemaphoreType.DMA((7,)),
+            pltpu.SemaphoreType.DMA((5,)),
         ],
         compiler_params=pltpu.CompilerParams(vmem_limit_bytes=VMEM_LIMIT),
         name="tiles",

time: 84.6 us -> 82.6 us (0.976)
  the two profiles are of different devices: /device:TPU:65 before, /device:TPU:1 now
where the time goes in v7:
time: 82.6 us; the launch traced here: 81.7 us
  Pallas kernels  81 us (98%)
    pallas_call x1, Pallas kernels, gather(): pl.pallas_call(gather_kernel, out_shape=tuple((jax.ShapeDtypeStruct(shape...  32 us
    pallas_call x1, Pallas kernels, scatter(): pl.pallas_call(scatter_kernel, out_shape=(jax.ShapeDtypeStruct((ROWS, 204...  31.5 us
    pallas_call x1, Pallas kernels, tiles(): pl.pallas_call(tile_kernel, out_shape=(jax.ShapeDtypeStruct((2, 8, QT, HD...  15.4 us
    pallas_call x1, Pallas kernels, store(): pl.pallas_call(store_kernel, out_shape=tuple((jax.ShapeDtypeStruct(array....  2.05 us

profile of v7, /device:TPU:1, one launch (start us, length us, event | category | flops | bytes accessed | tf_op | source)
XLA Modules:
  0.0 81.7 jit_solution(7481973453973607222)
XLA Ops:
  0.6 32.0 %gather_heads.1 = (bf16[8,256,256]{2,1,0:T(8,128)(2,1)}, bf16[8,256,256]{2,1,0:T(8,128)(2,1)}, f32[16,8,128]{2,1,0:T(8,128)}, bf16[4,2,2,256,256]{4,3,2,1,0:T(8,128)(2,1)}) custom-call(bf16[128,2048]{1,0:T(8,128)(2,1)} %q_ref.1, bf16[128,1024]{1,0:T(8,128)(2,1)} %k_ref.1, bf16[128,1024]{1,0:T(8,128)(2,1)} %v_ref.1, bf16[128,2048]{1,0:T(8,128)(2,1)} %o_ref.1, ...), custom_call_target="tpu_custom_call" | custom-call | tf_op jit(solution)/shard_map/gather_heads/pallas_call | solution.py:223
  32.6 15.4 %tiles.1 = (bf16[2,8,256,128]{3,2,1,0:T(8,128)(2,1)}, bf16[4,4,2,128,256]{4,3,2,1,0:T(8,128)(2,1)}) custom-call(s32[16]{0:T(128)} %order_ref.1, s32[4]{0:T(128)} %lens_ref.1, bf16[8,256,256]{2,1,0:T(8,128)(2,1)} %get-tuple-element.12.qh_ref, bf16[8,256,256]{2,1,0:T(8,128)(2,1)} %get-tuple-element.13.gh_ref, f32[16,8,128]{2,1,0:T(8,128)} %get-tuple-element.14.aux_ref, ...), custom_call_target="tpu_custom_call" | custom-call | tf_op jit(solution)/shard_map/tiles/pallas_call | solution.py:436
  48.1 31.5 %scatter_grads.1 = (bf16[128,2048]{1,0:T(8,128)(2,1)}, bf16[128,1024]{1,0:T(8,128)(2,1)}, bf16[128,1024]{1,0:T(8,128)(2,1)}) custom-call(bf16[2,8,256,128]{3,2,1,0:T(8,128)(2,1)} %get-tuple-element.16.dq_ref, bf16[4,4,2,128,256]{4,3,2,1,0:T(8,128)(2,1)} %get-tuple-element.17.dkv_ref), custom_call_target="tpu_custom_call" | custom-call | tf_op jit(solution)/shard_map/scatter_grads/pallas_call | solution.py:576
  79.6 2.1 %store_grads.1 = (bf16[128,2048]{1,0:T(8,128)(2,1)}, bf16[128,1024]{1,0:T(8,128)(2,1)}, bf16[128,1024]{1,0:T(8,128)(2,1)}) custom-call(bf16[128,2048]{1,0:T(8,128)(2,1)} %get-tuple-element.18.refs_0_, bf16[128,1024]{1,0:T(8,128)(2,1)} %get-tuple-element.19.refs_1_, bf16[128,1024]{1,0:T(8,128)(2,1)} %get-tuple-element.20.refs_2_), custom_call_target="tpu_custom_call" | custom-call | tf_op jit(solution)/shard_map/store_grads/pallas_call | solution.py:623

commit v8 on v7

--- a/solution.py
+++ b/solution.py
@@ -362,7 +362,7 @@
             p_ref[r : r + step, :] = p.astype(BF16)
             ds_ref[r : r + step, :] = ds.astype(BF16)
 
-        return [partial(score, 0), partial(score, 1)] + [partial(piece, r) for r in range(0, 2 * QT, step)]
+        return [partial(score, 0)] + [partial(piece, r) for r in range(0, QT // 2, step)] + [partial(score, 1)] + [partial(piece, r) for r in range(QT // 2, 2 * QT, step)]
 
     def gradients(t, p_ref, ds_ref):
         i, slot = tile_list[t] % 8, tile_list[t] // 8
@@ -399,13 +399,16 @@
         pl.when(jnp.logical_not(whole))(lambda: steps(True))
         return 0
 
-    for kind, (whole, turned) in enumerate(((q_v, qt_v), (g_v, gt_v))):
-        loads[1 + kind].wait()
-        for i in range(8):
-            for h in range(2):
-                turned[i, :, h * QT : (h + 1) * QT] = whole[i, :, h * HD : (h + 1) * HD].T
-    loads[3].wait()
-    run(weigh(0, p_a, ds_a, True))
+    def turn(whole, turned, i):
+        for h in range(2):
+            turned[i, :, h * QT : (h + 1) * QT] = whole[i, :, h * HD : (h + 1) * HD].T
+
+    for load in loads[1:]:
+        load.wait()
+    run(
+        weigh(0, p_a, ds_a, True),
+        [partial(turn, whole, turned, i) for whole, turned in ((q_v, qt_v), (g_v, gt_v)) for i in range(8)],
+    )
 
     lax.fori_loop(0, pairs, pair, 0)
 

time: 82.6 us -> 82.7 us (level)
  the two profiles are of different devices: /device:TPU:1 before, /device:TPU:72 now
where the time goes in v8:
time: 82.7 us; the launch traced here: 82.9 us
  Pallas kernels  82.3 us (100%)
    pallas_call x1, Pallas kernels, scatter(): pl.pallas_call(scatter_kernel, out_shape=(jax.ShapeDtypeStruct((ROWS, 204...  31.3 us
    pallas_call x1, Pallas kernels, gather(): pl.pallas_call(gather_kernel, out_shape=tuple((jax.ShapeDtypeStruct(shape...  30.1 us
    pallas_call x1, Pallas kernels, tiles(): pl.pallas_call(tile_kernel, out_shape=(jax.ShapeDtypeStruct((2, 8, QT, HD...  18.8 us
    pallas_call x1, Pallas kernels, store(): pl.pallas_call(store_kernel, out_shape=tuple((jax.ShapeDtypeStruct(array....  2.05 us

profile of v8, /device:TPU:72, one launch (start us, length us, event | category | flops | bytes accessed | tf_op | source)
XLA Modules:
  0.0 82.9 jit_solution(7262163058346829013)
XLA Ops:
  0.6 30.1 %gather_heads.1 = (bf16[8,256,256]{2,1,0:T(8,128)(2,1)}, bf16[8,256,256]{2,1,0:T(8,128)(2,1)}, f32[16,8,128]{2,1,0:T(8,128)}, bf16[4,2,2,256,256]{4,3,2,1,0:T(8,128)(2,1)}) custom-call(bf16[128,2048]{1,0:T(8,128)(2,1)} %q_ref.1, bf16[128,1024]{1,0:T(8,128)(2,1)} %k_ref.1, bf16[128,1024]{1,0:T(8,128)(2,1)} %v_ref.1, bf16[128,2048]{1,0:T(8,128)(2,1)} %o_ref.1, ...), custom_call_target="tpu_custom_call" | custom-call | tf_op jit(solution)/shard_map/gather_heads/pallas_call | solution.py:223
  30.8 18.8 %tiles.1 = (bf16[2,8,256,128]{3,2,1,0:T(8,128)(2,1)}, bf16[4,4,2,128,256]{4,3,2,1,0:T(8,128)(2,1)}) custom-call(s32[16]{0:T(128)} %order_ref.1, s32[4]{0:T(128)} %lens_ref.1, bf16[8,256,256]{2,1,0:T(8,128)(2,1)} %get-tuple-element.12.qh_ref, bf16[8,256,256]{2,1,0:T(8,128)(2,1)} %get-tuple-element.13.gh_ref, f32[16,8,128]{2,1,0:T(8,128)} %get-tuple-element.14.aux_ref, ...), custom_call_target="tpu_custom_call" | custom-call | tf_op jit(solution)/shard_map/tiles/pallas_call | solution.py:439
  49.6 31.3 %scatter_grads.1 = (bf16[128,2048]{1,0:T(8,128)(2,1)}, bf16[128,1024]{1,0:T(8,128)(2,1)}, bf16[128,1024]{1,0:T(8,128)(2,1)}) custom-call(bf16[2,8,256,128]{3,2,1,0:T(8,128)(2,1)} %get-tuple-element.16.dq_ref, bf16[4,4,2,128,256]{4,3,2,1,0:T(8,128)(2,1)} %get-tuple-element.17.dkv_ref), custom_call_target="tpu_custom_call" | custom-call | tf_op jit(solution)/shard_map/scatter_grads/pallas_call | solution.py:579
  80.9 2.1 %store_grads.1 = (bf16[128,2048]{1,0:T(8,128)(2,1)}, bf16[128,1024]{1,0:T(8,128)(2,1)}, bf16[128,1024]{1,0:T(8,128)(2,1)}) custom-call(bf16[128,2048]{1,0:T(8,128)(2,1)} %get-tuple-element.18.refs_0_, bf16[128,1024]{1,0:T(8,128)(2,1)} %get-tuple-element.19.refs_1_, bf16[128,1024]{1,0:T(8,128)(2,1)} %get-tuple-element.20.refs_2_), custom_call_target="tpu_custom_call" | custom-call | tf_op jit(solution)/shard_map/store_grads/pallas_call | solution.py:626

commit v9 on v8

--- a/solution.py
+++ b/solution.py
@@ -508,6 +508,19 @@
                 dkv_ref.at[1 + 2 * way, slot[h], part], land1.at[way, part, h], s1_send.at[at], s1_recv.at[at], to
             )
 
+    for load in loads:
+        load.wait()
+    for h in SLOTS:
+        for way, to in enumerate(ways):
+            part = way
+            copies2[part, h].wait_recv()
+            total = own[1 + 2 * way, slot[h], part].astype(F32) + land2[part, h].astype(F32)
+            send1[way, h] = total.astype(BF16)
+            at = (way * 2 + part) * 4 + h
+            copies1[way, part, h] = send(
+                send1.at[way, h], land1.at[way, part, h], s1_send.at[at], s1_recv.at[at], to
+            )
+
     mine_load.wait()
     sib_copy.wait_recv()
     q_copies = []
@@ -526,19 +539,6 @@
                 q_copies.append((True, copy))
             else:
                 q_copies.append((False, send(src, dst, q_send.at[at], q_recv.at[at], device(tx, tz, y, tc))))
-
-    for load in loads:
-        load.wait()
-    for h in SLOTS:
-        for way, to in enumerate(ways):
-            part = way
-            copies2[part, h].wait_recv()
-            total = own[1 + 2 * way, slot[h], part].astype(F32) + land2[part, h].astype(F32)
-            send1[way, h] = total.astype(BF16)
-            at = (way * 2 + part) * 4 + h
-            copies1[way, part, h] = send(
-                send1.at[way, h], land1.at[way, part, h], s1_send.at[at], s1_recv.at[at], to
-            )
 
     f_copies = []
 

time: 82.7 us -> 83 us (level)
  the two profiles are of different devices: /device:TPU:72 before, /device:TPU:1 now
where the time goes in v9:
time: 83 us; the launch traced here: 81.4 us
  Pallas kernels  80.7 us (97%)
    pallas_call x1, Pallas kernels, gather(): pl.pallas_call(gather_kernel, out_shape=tuple((jax.ShapeDtypeStruct(shape...  32 us
    pallas_call x1, Pallas kernels, scatter(): pl.pallas_call(scatter_kernel, out_shape=(jax.ShapeDtypeStruct((ROWS, 204...  29.6 us
    pallas_call x1, Pallas kernels, tiles(): pl.pallas_call(tile_kernel, out_shape=(jax.ShapeDtypeStruct((2, 8, QT, HD...  17.1 us
    pallas_call x1, Pallas kernels, store(): pl.pallas_call(store_kernel, out_shape=tuple((jax.ShapeDtypeStruct(array....  2.05 us

profile of v9, /device:TPU:1, one launch (start us, length us, event | category | flops | bytes accessed | tf_op | source)
XLA Modules:
  0.0 81.4 jit_solution(4389680333944024976)
XLA Ops:
  0.6 32.0 %gather_heads.1 = (bf16[8,256,256]{2,1,0:T(8,128)(2,1)}, bf16[8,256,256]{2,1,0:T(8,128)(2,1)}, f32[16,8,128]{2,1,0:T(8,128)}, bf16[4,2,2,256,256]{4,3,2,1,0:T(8,128)(2,1)}) custom-call(bf16[128,2048]{1,0:T(8,128)(2,1)} %q_ref.1, bf16[128,1024]{1,0:T(8,128)(2,1)} %k_ref.1, bf16[128,1024]{1,0:T(8,128)(2,1)} %v_ref.1, bf16[128,2048]{1,0:T(8,128)(2,1)} %o_ref.1, ...), custom_call_target="tpu_custom_call" | custom-call | tf_op jit(solution)/shard_map/gather_heads/pallas_call | solution.py:223
  32.6 17.1 %tiles.1 = (bf16[2,8,256,128]{3,2,1,0:T(8,128)(2,1)}, bf16[4,4,2,128,256]{4,3,2,1,0:T(8,128)(2,1)}) custom-call(s32[16]{0:T(128)} %order_ref.1, s32[4]{0:T(128)} %lens_ref.1, bf16[8,256,256]{2,1,0:T(8,128)(2,1)} %get-tuple-element.12.qh_ref, bf16[8,256,256]{2,1,0:T(8,128)(2,1)} %get-tuple-element.13.gh_ref, f32[16,8,128]{2,1,0:T(8,128)} %get-tuple-element.14.aux_ref, ...), custom_call_target="tpu_custom_call" | custom-call | tf_op jit(solution)/shard_map/tiles/pallas_call | solution.py:439
  49.8 29.6 %scatter_grads.1 = (bf16[128,2048]{1,0:T(8,128)(2,1)}, bf16[128,1024]{1,0:T(8,128)(2,1)}, bf16[128,1024]{1,0:T(8,128)(2,1)}) custom-call(bf16[2,8,256,128]{3,2,1,0:T(8,128)(2,1)} %get-tuple-element.16.dq_ref, bf16[4,4,2,128,256]{4,3,2,1,0:T(8,128)(2,1)} %get-tuple-element.17.dkv_ref), custom_call_target="tpu_custom_call" | custom-call | tf_op jit(solution)/shard_map/scatter_grads/pallas_call | solution.py:579
  79.3 2.1 %store_grads.1 = (bf16[128,2048]{1,0:T(8,128)(2,1)}, bf16[128,1024]{1,0:T(8,128)(2,1)}, bf16[128,1024]{1,0:T(8,128)(2,1)}) custom-call(bf16[128,2048]{1,0:T(8,128)(2,1)} %get-tuple-element.18.refs_0_, bf16[128,1024]{1,0:T(8,128)(2,1)} %get-tuple-element.19.refs_1_, bf16[128,1024]{1,0:T(8,128)(2,1)} %get-tuple-element.20.refs_2_), custom_call_target="tpu_custom_call" | custom-call | tf_op jit(solution)/shard_map/store_grads/pallas_call | solution.py:626
